TPU v7x, 32 devices: a whole 2x2x4 slice. The times are simulated.
32 devices in a mesh: seq: 8 (over y, x, core), grp: 4 (over z).
Axes of the slice: x: 2, y: 2, z: 4, core: 2. Of those that a mesh axis runs over, the one named last changes fastest.
Arguments:
- tokens: bfloat16 [768, 32768], P('grp', 'seq'), may hold values from -6 to 6
- cotangent: bfloat16 [768, 32768], P('grp', 'seq'), may hold values from -6 to 6
- lengths: int32 [64], P('seq'), may hold values from 64 to 512, as said below
- w_query: bfloat16 [768, 192], P('grp'), may hold values from -0.4375 to 0.4375
- w_key: bfloat16 [768, 192], P('grp'), may hold values from -0.4375 to 0.4375
- w_value: bfloat16 [768, 192], P('grp'), may hold values from -0.4375 to 0.4375
- b_query: float32 [768], P('grp'), may hold values from -3 to 3
- b_value: float32 [768], P('grp'), may hold values from -3 to 3
- w_out: bfloat16 [768, 768], P('grp'), may hold values from -1.75 to 1.75
- b_out: float32 [768], P('grp'), may hold values from -3 to 3
- gain_attn: float32 [768], P('grp'), may hold values from 0.5 to 1.5
- shift_attn: float32 [768], P('grp'), may hold values from -3 to 3
- w_inter: bfloat16 [768, 768], P('grp'), may hold values from -0.4375 to 0.4375
- b_inter: float32 [3072], P('grp'), may hold values from -3 to 3
- w_back: bfloat16 [768, 768], P('grp'), may hold values from -0.21875 to 0.21875
- b_back: float32 [768], P('grp'), may hold values from -3 to 3
- gain_ffn: float32 [768], P('grp'), may hold values from 0.5 to 1.5
- shift_ffn: float32 [768], P('grp'), may hold values from -3 to 3
Outputs:
- result: bfloat16 [768, 32768], P('grp', 'seq')
- grad_tokens: float32 [768, 32768], P('grp', 'seq')
- grad_w_query: float32 [768, 192], P('grp')
- grad_w_key: float32 [768, 192], P('grp')
- grad_w_value: float32 [768, 192], P('grp')
- grad_b_query: float32 [768], P('grp')
- grad_b_value: float32 [768], P('grp')
- grad_w_out: float32 [768, 768], P('grp')
- grad_b_out: float32 [768], P('grp')
- grad_gain_attn: float32 [768], P('grp')
- grad_shift_attn: float32 [768], P('grp')
- grad_w_inter: float32 [768, 768], P('grp')
- grad_b_inter: float32 [3072], P('grp')
- grad_w_back: float32 [768, 768], P('grp')
- grad_b_back: float32 [768], P('grp')
- grad_gain_ffn: float32 [768], P('grp')
- grad_shift_ffn: float32 [768], P('grp')
Inputs may be any that keep to these rules, and one draw needn't show every extreme that they name: `lengths`: slots of a sequence at or past its length are padding; some sequence has 512 tokens and some has 64.
All inputs are finite; a program needn't handle non-finite values.
Results may differ from a plain program's by a relative error of at most 0.013.
Values may be sent and summed in bfloat16 or wider, within the bound.
A program may use at most 128 MiB of HBM per device.

v0:
```python
from functools import partial
import math

import jax
import jax.numpy as jnp
from jax import lax
from jax.sharding import PartitionSpec as P

HEAD_DIM = 64


eps_norm = 1e-12


def matmul(left, right):
    return jnp.dot(left, right, preferred_element_type=jnp.float32)


def inner_rows(left, right):
    return lax.dot_general(
        left, right, (((0,), (0,)), ((), ())), preferred_element_type=jnp.float32
    )


def times_back(left, right):
    return lax.dot_general(
        left, right, (((1,), (1,)), ((), ())), preferred_element_type=jnp.float32
    )


def layer_norm(resid, gain, shift):
    width = resid.shape[0] * lax.axis_size("grp")
    total, squares = lax.psum((jnp.sum(resid, axis=0), jnp.sum(resid * resid, axis=0)), "grp")
    center_mean = total / width
    spread = squares / width - center_mean * center_mean
    scale_inv = lax.rsqrt(spread + eps_norm)
    normed = (resid - center_mean[None, :]) * scale_inv[None, :]
    return (normed * gain[:, None] + shift[:, None], normed, scale_inv)


def norm_back(grad_out, normed, scale_inv, gain):
    width = grad_out.shape[0] * lax.axis_size("grp")
    scaled = grad_out * gain[:, None]
    first, second = lax.psum((jnp.sum(scaled, axis=0), jnp.sum(scaled * normed, axis=0)), "grp")
    grad_in = scale_inv[None, :] * (
        scaled - first[None, :] / width - normed * (second[None, :] / width)
    )
    return (grad_in, jnp.sum(grad_out * normed, axis=1), jnp.sum(grad_out, axis=1))


def masked_scores(queries, key_rows, length):
    factor = 1.0 / math.sqrt(queries.shape[1])
    scores = (
        jnp.einsum("heq,hek->hqk", queries, key_rows, preferred_element_type=jnp.float32) * factor
    )
    places = jnp.arange(key_rows.shape[2], dtype=jnp.int32)
    return jnp.where((places < length)[None, None, :], scores, -1e30)


def attend_seq(packed):
    queries, key_rows, val_rows, length = packed
    scores = masked_scores(queries, key_rows, length)
    top = jnp.max(scores, axis=-1, keepdims=True)
    expo = jnp.exp(scores - top)
    total = jnp.sum(expo, axis=-1, keepdims=True)
    probs = (expo / total).astype(jnp.bfloat16)
    context = jnp.einsum("hqk,hek->heq", probs, val_rows, preferred_element_type=jnp.float32)
    return (context.astype(jnp.bfloat16), top[..., 0] + jnp.log(total[..., 0]))


def attend_back(packed):
    queries, key_rows, val_rows, length, logsum, grad_ctx = packed
    factor = 1.0 / math.sqrt(queries.shape[1])
    scores = masked_scores(queries, key_rows, length)
    probs = jnp.exp(scores - logsum[..., None])
    grad_probs = jnp.einsum("heq,hek->hqk", grad_ctx, val_rows, preferred_element_type=jnp.float32)
    delta = jnp.sum(probs * grad_probs, axis=-1, keepdims=True)
    grad_scores = (probs * (grad_probs - delta) * factor).astype(jnp.bfloat16)
    grad_q = jnp.einsum("hqk,hek->heq", grad_scores, key_rows, preferred_element_type=jnp.float32)
    grad_k = jnp.einsum("hqk,heq->hek", grad_scores, queries, preferred_element_type=jnp.float32)
    grad_v = jnp.einsum(
        "hqk,heq->hek", probs.astype(jnp.bfloat16), grad_ctx, preferred_element_type=jnp.float32
    )
    return (grad_q.astype(jnp.bfloat16), grad_k.astype(jnp.bfloat16), grad_v.astype(jnp.bfloat16))


def local(
    tokens,
    cotangent,
    lengths,
    w_query,
    w_key,
    w_value,
    b_query,
    b_value,
    w_out,
    b_out,
    gain_attn,
    shift_attn,
    w_inter,
    b_inter,
    w_back,
    b_back,
    gain_ffn,
    shift_ffn,
):
    group_width, rows = tokens.shape
    seq_count = lengths.shape[0]
    seq_len = rows // seq_count
    head_count = group_width // HEAD_DIM

    def to_seqs(flat):
        return jnp.transpose(flat.reshape(head_count, HEAD_DIM, seq_count, seq_len), (2, 0, 1, 3))

    def from_seqs(stacked):
        return jnp.transpose(stacked, (1, 2, 0, 3)).reshape(group_width, rows)

    queries = (inner_rows(w_query, tokens) + b_query[:, None]).astype(jnp.bfloat16)
    key_rows = inner_rows(w_key, tokens).astype(jnp.bfloat16)
    val_rows = (inner_rows(w_value, tokens) + b_value[:, None]).astype(jnp.bfloat16)
    queries_four = to_seqs(queries)
    keys_four = to_seqs(key_rows)
    values_four = to_seqs(val_rows)
    context, logsum = lax.map(attend_seq, (queries_four, keys_four, values_four, lengths))
    context_flat = from_seqs(context)
    gathered = lax.all_gather(context_flat, "grp", axis=0, tiled=True)
    branch_raw = matmul(w_out, gathered)
    branch = branch_raw + b_out[:, None]
    middle, normed_attn, inv_attn = layer_norm(
        tokens.astype(jnp.float32) + branch, gain_attn, shift_attn
    )
    middle_low = middle.astype(jnp.bfloat16)
    inner = inner_rows(w_inter, middle_low) + b_inter[:, None]
    gelu_exact = partial(jax.nn.gelu, approximate=False)
    active_f, gelu_pull = jax.vjp(gelu_exact, inner)
    active = active_f.astype(jnp.bfloat16)
    ffn_out = matmul(w_back, active) + b_back[:, None]
    final, normed_ffn, inv_ffn = layer_norm(middle + ffn_out, gain_ffn, shift_ffn)
    result = final.astype(jnp.bfloat16)
    grad_r2, grad_gain_ffn, grad_shift_ffn = norm_back(
        cotangent.astype(jnp.float32), normed_ffn, inv_ffn, gain_ffn
    )
    grad_ffn = grad_r2.astype(jnp.bfloat16)
    grad_b_back = jnp.sum(grad_ffn.astype(jnp.float32), axis=1)
    grad_w_back = times_back(grad_ffn, active)
    grad_active = inner_rows(w_back, grad_ffn)
    grad_inner = gelu_pull(grad_active)[0].astype(jnp.bfloat16)
    grad_b_inter = jnp.sum(grad_inner.astype(jnp.float32), axis=1)
    grad_w_inter = times_back(middle_low, grad_inner)
    grad_mid = grad_r2 + matmul(w_inter, grad_inner)
    grad_r1, grad_gain_attn, grad_shift_attn = norm_back(grad_mid, normed_attn, inv_attn, gain_attn)
    grad_branch = grad_r1.astype(jnp.bfloat16)
    grad_b_out = jnp.sum(grad_branch.astype(jnp.float32), axis=1)
    grad_w_out = times_back(grad_branch, gathered)
    context_terms = inner_rows(w_out, grad_branch)
    grad_context = lax.psum_scatter(context_terms, "grp", scatter_dimension=0, tiled=True).astype(
        jnp.bfloat16
    )
    grad_q, grad_k, grad_v = lax.map(
        attend_back, (queries_four, keys_four, values_four, lengths, logsum, to_seqs(grad_context))
    )
    grad_q = from_seqs(grad_q)
    grad_k = from_seqs(grad_k)
    grad_v = from_seqs(grad_v)
    grad_b_query = jnp.sum(grad_q.astype(jnp.float32), axis=1)
    grad_b_value = jnp.sum(grad_v.astype(jnp.float32), axis=1)
    grad_w_query = times_back(tokens, grad_q)
    grad_w_key = times_back(tokens, grad_k)
    grad_w_value = times_back(tokens, grad_v)
    grad_tokens = (
        grad_r1 + matmul(w_query, grad_q) + matmul(w_key, grad_k) + matmul(w_value, grad_v)
    )
    (
        grad_w_query,
        grad_w_key,
        grad_w_value,
        grad_b_query,
        grad_b_value,
        grad_w_out,
        grad_b_out,
        grad_gain_attn,
        grad_shift_attn,
        grad_w_inter,
        grad_b_inter,
        grad_w_back,
        grad_b_back,
        grad_gain_ffn,
        grad_shift_ffn,
    ) = lax.psum(
        (
            grad_w_query,
            grad_w_key,
            grad_w_value,
            grad_b_query,
            grad_b_value,
            grad_w_out,
            grad_b_out,
            grad_gain_attn,
            grad_shift_attn,
            grad_w_inter,
            grad_b_inter,
            grad_w_back,
            grad_b_back,
            grad_gain_ffn,
            grad_shift_ffn,
        ),
        "seq",
    )
    return (
        result,
        grad_tokens,
        grad_w_query,
        grad_w_key,
        grad_w_value,
        grad_b_query,
        grad_b_value,
        grad_w_out,
        grad_b_out,
        grad_gain_attn,
        grad_shift_attn,
        grad_w_inter,
        grad_b_inter,
        grad_w_back,
        grad_b_back,
        grad_gain_ffn,
        grad_shift_ffn,
    )


def solution(mesh):
    placed = (
        P("grp", "seq"),
        P("grp", "seq"),
        P("seq"),
        P("grp", None),
        P("grp", None),
        P("grp", None),
        P("grp"),
        P("grp"),
        P("grp", None),
        P("grp"),
        P("grp"),
        P("grp"),
        P("grp", None),
        P("grp"),
        P("grp", None),
        P("grp"),
        P("grp"),
        P("grp"),
    )
    return jax.shard_map(
        local,
        mesh=mesh,
        in_specs=placed,
        out_specs=(
            P("grp", "seq"),
            P("grp", "seq"),
            P("grp", None),
            P("grp", None),
            P("grp", None),
            P("grp"),
            P("grp"),
            P("grp", None),
            P("grp"),
            P("grp"),
            P("grp"),
            P("grp", None),
            P("grp"),
            P("grp", None),
            P("grp"),
            P("grp"),
            P("grp"),
        ),
        check_vma=False,
    )
```

profile of v0, /device:TPU:0, one launch (start us, length us, event | category | flops | bytes accessed | tf_op | source)
XLA Modules:
  0.0 822.0 jit_solution(7647561425713530891)
XLA Ops:
  19.7 50.0 %while.26 = (s32[]{:T(128)}, bf16[8,3,64,512]{3,2,1,0:T(8,128)(2,1)S(1)}, f32[8,3,512]{2,1,0:T(4,128)}, bf16[8,3,64,512]{3,2,1,0:T(8,128)(2,1)}, s32[8]{0:T(128)...) while((s32[]{:T(128)}, bf16[8,3,64,512]{3,2,1,0:T(8,128)(2,1)S(1)}, ...), condition=%wide.region_3.4_spmd, body=%wide.region_0.3_spmd.sunk | while | flops 210861056 | bytes 10283621 | solution.py:124
  72.5 118.1 %all-gather.2.cloned.1.call-done = bf16[768,4096]{1,0:T(8,128)(2,1)} async-done(((bf16[192,4096]{1,0:T(8,128)(2,1)}), bf16[768,4096]{1,0:T(8,128)(2,1)}) %all-gather.2.cloned.1.call-update) | async-done | bytes 6291472 | tf_op jit(solution)/shard_map/all_gather | solution.py:126
  190.7 6.1 fusion.131
  196.8 16.3 %all-reduce.5 = (f32[4096]{0:T(1024)S(1)}, f32[4096]{0:T(1024)S(1)}) all-reduce(f32[4096]{0:T(1024)S(1)} %get-tuple-element.221, f32[4096]{0:T(1024)S(1)} %get-tuple-element.220), channel_id=1, replica_groups=mesh['seq'=8,'grp'=4] {'grp'}, use_global_device_ids=true, to_apply=%region_7.8 | all-reduce | flops 8192 | bytes 65536 | tf_op jit(solution)/shard_map/psum | solution.py:33
  213.2 32.4 %fusion.91 = (bf16[768,4096]{0,1:T(8,128)(2,1)S(1)}, f32[768,4096]{0,1:T(8,128)}, f32[4096,768]{1,0:T(8,128)}) fusion(f32[768]{0:T(1024)S(1)} %copy-done.35, bf16[192,768]{1,0:T(8,128)(2,1)S(1)} %copy-done, f32[192,4096]{1,0:T(8,128)} %get-tuple-element.294, f32[192]{0:T(256)S(1)} %copy-done.39, f32[192]{0:T(256)S(1)} %copy-done.31, ...), kind=kOutput, calls=%fused_computation.85 | convolution fusion | flops 1419509760 | bytes 34935296 | tf_op jit(solution)/shard_map/dot_general | solution.py:20
  248.3 17.2 %all-reduce.4 = (f32[4096]{0:T(1024)S(1)}, f32[4096]{0:T(1024)S(1)}) all-reduce(f32[4096]{0:T(1024)S(1)} %get-tuple-element.219, f32[4096]{0:T(1024)S(1)} %get-tuple-element.218), channel_id=1, replica_groups=mesh['seq'=8,'grp'=4] {'grp'}, use_global_device_ids=true, to_apply=%region_11.12 | all-reduce | flops 8192 | bytes 65536 | tf_op jit(solution)/shard_map/psum | solution.py:33
  265.6 5.0 fusion.120
  270.6 17.2 %all-reduce.3 = (f32[4096]{0:T(1024)}, f32[4096]{0:T(1024)S(1)}) all-reduce(f32[4096]{0:T(1024)S(1)} %get-tuple-element.215, f32[4096]{0:T(1024)S(1)} %get-tuple-element.222), channel_id=1, replica_groups=mesh['seq'=8,'grp'=4] {'grp'}, use_global_device_ids=true, to_apply=%region_15.16 | all-reduce | flops 8192 | bytes 65536 | tf_op jit(solution)/shard_map/psum | solution.py:44
  288.5 4.6 convert_reduce_fusion.2
  293.2 15.6 %convert_reduce_fusion = (f32[768]{0:T(1024)S(1)}, bf16[768,4096]{0,1:T(8,128)(2,1)}) fusion(f32[768,4096]{0,1:T(8,128)} %get-tuple-element.286, bf16[192,4096]{1,0:T(8,128)(2,1)S(1)} %get-tuple-element.282, bf16[192,768]{1,0:T(8,128)(2,1)S(1)} %copy-done.34, f32[4096,768]{1,0:T(8,128)} %get-tuple-element.295, f32[768]{0:T(1024)S(1)} %copy-done.36), kind=kOutput, calls=%fused_computation.86 | convolution fusion | flops 1261436160 | bytes 33331200 | tf_op jit(solution)/shard_map/dot_general | solution.py:20
  308.8 8.0 multiply_reduce_fusion.1
  316.8 17.2 %all-reduce.2 = (f32[4096]{0:T(1024)S(1)}, f32[4096]{0:T(1024)S(1)}) all-reduce(f32[4096]{0:T(1024)S(1)} %get-tuple-element.213, f32[4096]{0:T(1024)S(1)} %get-tuple-element.216), channel_id=1, replica_groups=mesh['seq'=8,'grp'=4] {'grp'}, use_global_device_ids=true, to_apply=%region_19.20 | all-reduce | flops 8192 | bytes 65536 | tf_op jit(solution)/shard_map/psum | solution.py:44
  334.0 4.5 convert_reduce_fusion.3
  338.6 6.3 convolution_bitcast_fusion
  344.9 12.6 %copy.98 = f32[768,4096]{1,0:T(8,128)} copy(f32[768,4096]{0,1:T(8,128)} %convolution_bitcast_fusion) | data formatting | bytes 25165824
  357.8 5.5 fusion.134
  363.3 6.0 fusion.123
  369.3 5.2 fusion.126
  374.5 193.2 %reduce-scatter.4.cloned.1.call-done = f32[192,4096]{1,0:T(8,128)} async-done(((f32[768,4096]{1,0:T(8,128)}), f32[192,4096]{1,0:T(8,128)}) %reduce-scatter.4.cloned.1.call-update) | async-done | bytes 3145744 | tf_op jit(solution)/shard_map/reduce_scatter | solution.py:156
  576.2 148.9 %while.27 = (s32[]{:T(128)}, bf16[8,3,64,512]{3,2,1,0:T(8,128)(2,1)}, bf16[8,3,64,512]{3,2,1,0:T(8,128)(2,1)}, bf16[8,3,64,512]{3,2,1,0:T(8,128)(2,1)}, bf16[8,3...) while((s32[]{:T(128)}, ...), condition=%wide.region_23.24_spmd, body=%wide.region_21.23_spmd.sunk | while | flops 514626048 | bytes 36593792 | solution.py:159
  588.0 4.7 fusion.200
  606.6 4.7 fusion.200
  625.2 4.7 fusion.200
  639.3 4.6 fusion.201
  643.8 4.7 fusion.200
  662.4 4.6 fusion.200
  681.0 4.6 fusion.200
  695.0 4.5 fusion.201
  699.6 4.7 fusion.200
  718.2 4.7 fusion.200
  739.6 25.0 %all-reduce = (f32[192]{0:T(256)}, f32[192]{0:T(256)}, f32[192]{0:T(256)}, f32[192]{0:T(256)}, f32[192]{0:T(256)}, /*index=5*/f32[768]{0:T(1024)}, f32[192]{0:T(256)}, f32[192]{0:T(256)}, f32[192]{0:T(256)}) all-reduce(f32[192]{0:T(256)} %reduce_sum.184, f32[192]{0:T(256)} %reduce_sum.186, ...), channel_id=1, replica_groups=mesh['seq'=8,'grp'=4] {'seq'}, use_global_device_ids=true, to_apply=%region_28.29 | all-reduce | flops 2304 | bytes 18432 | tf_op jit(solution)/shard_map/psum | solution.py:189
  770.5 34.8 %all-reduce.8.cloned.1.call-done = (f32[192,192]{0,1:T(8,128)}, f32[192,192]{0,1:T(8,128)}, f32[192,192]{0,1:T(8,128)}, f32[192,768]{1,0:T(8,128)}, f32[192,768]{1,0:T(8,128)}, /*index=5*/f32[192,768]{1,0:T(8,128)}) async-done(((f32[192,192]{0,1:T(8,128)}, f32[192,192]{0,1:T(8,128)}, f32[192,192]{0,1:T(8,128)}, f32[192,768]{1,0:T(8,128)}, f32[192,768]{1,0:T(8,128)}, /*index=5*/f32[192,768]{1,0:T(8,128)}), ...) | async-done | bytes 2211856 | tf_op jit(solution)/shard_map/psum | solution.py:189
  (244 shorter events, 209.5 us)
Async XLA Ops:
  7.2 205.9 %copy-start = (bf16[192,768]{1,0:T(8,128)(2,1)S(1)}, bf16[192,768]{1,0:T(8,128)(2,1)}, u32[]{:S(2)}) copy-start(bf16[192,768]{1,0:T(8,128)(2,1)} %param.34) | copy-start | bytes 884740
  7.2 183.5 %all-gather.2.cloned.1.call-start = ((), (), s32[]{:S(2)}) async-start(), calls=%async_computation.1 | async-start | bytes 7864320 | tf_op jit(solution)/shard_map/all_gather | solution.py:126
  7.3 2.8 copy-start.3
  7.3 2.8 copy-start.20
  15.4 4.3 copy-start.41
  70.6 120.1 %copy-start.24 = (bf16[192,768]{1,0:T(8,128)(2,1)S(1)}, bf16[192,768]{1,0:T(8,128)(2,1)}, u32[]{:S(2)}) copy-start(bf16[192,768]{1,0:T(8,128)(2,1)} %param.30) | copy-start | bytes 884740
  70.6 120.1 %copy-start.37 = (f32[192]{0:T(256)S(1)}, f32[192]{0:T(256)}, u32[]{:S(2)}) copy-start(f32[192]{0:T(256)} %param.31) | copy-start | bytes 2308
  72.5 140.7 %copy-start.31 = (f32[192]{0:T(256)S(1)}, f32[192]{0:T(256)}, u32[]{:S(2)}) copy-start(f32[192]{0:T(256)} %param.32) | copy-start | bytes 2308
  72.5 140.7 %copy-start.35 = (f32[768]{0:T(1024)S(1)}, f32[768]{0:T(1024)}, u32[]{:S(2)}) copy-start(f32[768]{0:T(1024)} %param.35) | copy-start | bytes 9220
  72.5 140.7 %copy-start.39 = (f32[192]{0:T(256)S(1)}, f32[192]{0:T(256)}, u32[]{:S(2)}) copy-start(f32[192]{0:T(256)} %param.33) | copy-start | bytes 2308
  72.5 495.3 %reduce-scatter.4.cloned.1.call-start = ((), (), s32[]{:S(2)}) async-start(), calls=%async_computation.2 | async-start | bytes 15728640 | tf_op jit(solution)/shard_map/reduce_scatter | solution.py:156
  213.2 32.5 %copy-start.14 = (f32[192,4096]{1,0:T(8,128)S(1)}, f32[192,4096]{1,0:T(8,128)}, u32[]{:S(2)}) copy-start(f32[192,4096]{1,0:T(8,128)} %get-tuple-element.294) | copy-start | bytes 9437188
  213.2 32.5 %copy-start.33 = (bf16[192,768]{1,0:T(8,128)(2,1)S(1)}, bf16[192,768]{1,0:T(8,128)(2,1)}, u32[]{:S(2)}) copy-start(bf16[192,768]{1,0:T(8,128)(2,1)} %param.36) | copy-start | bytes 884740
  213.2 32.5 %copy-start.38 = (f32[192]{0:T(256)S(1)}, f32[192]{0:T(256)}, u32[]{:S(2)}) copy-start(f32[192]{0:T(256)} %param.37) | copy-start | bytes 2308
  245.7 19.9 %copy-start.26 = (f32[192]{0:T(256)S(1)}, f32[192]{0:T(256)}, u32[]{:S(2)}) copy-start(f32[192]{0:T(256)} %param.38) | copy-start | bytes 2308
  288.5 4.6 copy-start.34
  288.5 4.6 copy-start.36
  293.1 15.6 %copy-start.17 = (bf16[192,4096]{1,0:T(8,128)(2,1)}, bf16[192,4096]{1,0:T(8,128)(2,1)S(1)}, u32[]{:S(2)}) copy-start(bf16[192,4096]{1,0:T(8,128)(2,1)S(1)} %get-tuple-element.282) | copy-start | bytes 4718596
  293.1 15.6 %copy-start.13 = (bf16[192,4096]{1,0:T(8,128)(2,1)S(1)}, bf16[192,4096]{1,0:T(8,128)(2,1)}, u32[]{:S(2)}) copy-start(bf16[192,4096]{1,0:T(8,128)(2,1)} %param.23) | copy-start | bytes 4718596
  293.1 15.6 %copy-start.15 = (f32[192,4096]{1,0:T(8,128)S(1)}, f32[192,4096]{1,0:T(8,128)}, u32[]{:S(2)}) copy-start(f32[192,4096]{1,0:T(8,128)} %get-tuple-element.294) | copy-start | bytes 9437188
  293.1 15.6 %copy-start.27 = (f32[192]{0:T(256)S(1)}, f32[192]{0:T(256)}, u32[]{:S(2)}) copy-start(f32[192]{0:T(256)} %param.38) | copy-start | bytes 2308
  293.1 15.6 %copy-start.32 = (f32[192]{0:T(256)S(1)}, f32[192]{0:T(256)}, u32[]{:S(2)}) copy-start(f32[192]{0:T(256)} %param.32) | copy-start | bytes 2308
  334.0 4.6 copy-start.25
  338.6 24.7 %copy-start.1 = (f32[192,4096]{1,0:T(8,128)}, f32[192,4096]{1,0:T(8,128)S(1)}, u32[]{:S(2)}) copy-start(f32[192,4096]{1,0:T(8,128)S(1)} %get-tuple-element.284) | copy-start | bytes 9437188
  357.6 447.8 %all-reduce.8.cloned.1.call-start = ((), (), s32[]{:S(2)}) async-start(), calls=%async_computation.3 | async-start | bytes 4718592 | tf_op jit(solution)/shard_map/psum | solution.py:189
  363.3 6.0 copy-start.16
  363.3 6.0 copy-start.40
  572.3 4.0 copy-start.42
  725.1 4.8 copy-start.6
  737.2 27.4 %copy-start.2 = (f32[192,4096]{1,0:T(8,128)S(1)}, f32[192,4096]{1,0:T(8,128)}, u32[]{:S(2)}) copy-start(f32[192,4096]{1,0:T(8,128)} %copy-done.1) | copy-start | bytes 9437188
  737.2 27.4 %copy-start.19 = (bf16[192,192]{1,0:T(8,128)(2,1)S(1)}, bf16[192,192]{1,0:T(8,128)(2,1)}, u32[]{:S(2)}) copy-start(bf16[192,192]{1,0:T(8,128)(2,1)} %param.25) | copy-start | bytes 221188
  805.3 9.1 %copy-start.18 = (f32[192,768]{1,0:T(8,128)S(1)}, f32[192,768]{1,0:T(8,128)}, u32[]{:S(2)}) copy-start(f32[192,768]{1,0:T(8,128)} %get-tuple-element.480) | copy-start | bytes 1769476
  (15 other events, 30.6 us)
Sparse Core Ops, SparseCore 0:
  72.6 118.0 all-gather.1
  357.7 210.0 reduce-scatter.3
  739.7 65.5 all-reduce.7
where the time goes:
time: 832 us; the launch traced here: 822 us
  waiting for transfers between devices  346 us (42%)
  matrix products  262 us (31%)
  blocking collectives  92.9 us (11%)
  local copies, waits for them, and re-layouts  63.8 us (8%)
  other arithmetic  41.4 us (5%)
  between operations  14.6 us (2%)
    reduce_scatter x1, waiting for transfers between devices, local(): lax.psum_scatter(context_terms, 'grp', scatter_dimension=0, tiled=True)  193 us
    all_gather x1, waiting for transfers between devices, local(): gathered = lax.all_gather(context_flat, 'grp', axis=0, tiled=True)  118 us
    dot_general x6, matrix products, inner_rows(): lax.dot_general(left, right, (((0,), (0,)), ((), ())), preferred_element_...  57.7 us
    dot_general x8, matrix products, attend_back(): jnp.einsum('hqk,hek->heq', grad_scores, key_rows, preferred_element_type=...  37.3 us
    dot_general x8, matrix products, attend_back(): jnp.einsum('hqk,heq->hek', grad_scores, queries, preferred_element_type=j...  36.2 us
    psum x1, waiting for transfers between devices, local(): lax.psum((grad_w_query, grad_w_key, grad_w_value, grad_b_query, grad_b_va...  34.8 us
    psum x2, blocking collectives, norm_back(): lax.psum((jnp.sum(scaled, axis=0), jnp.sum(scaled * normed, axis=0)), 'grp')  34.4 us
    psum x2, blocking collectives, layer_norm(): lax.psum((jnp.sum(resid, axis=0), jnp.sum(resid * resid, axis=0)), 'grp')  33.5 us
  transfers between devices with their start and end apart: 3, of which 3 were waited for; matrix products, arithmetic and copies ran while one was open for 3% of the time, Pallas kernels for 0%

commit v1 on v0

v1 whole, which is shorter than its diff:
```python
import functools
import math

import jax
import jax.numpy as jnp
from jax import lax
from jax.experimental import pallas as pl
from jax.experimental.pallas import tpu as pltpu
from jax.sharding import PartitionSpec as P

HEAD_DIM = 64
EPS = 1e-12
MASKED = -1e30
F32, LOW = jnp.float32, jnp.bfloat16
VMEM_BYTES = 60 * 1024 * 1024
MESH = pl.DeviceIdType.MESH
BLOCK = 256
ERF_P = 0.3275911
ERF_A = (0.254829592, -0.284496736, 1.421413741, -1.453152027, 1.061405429)
B_QUERY, B_VALUE, B_OUT, GAIN1, SHIFT1, B_BACK, GAIN2, SHIFT2, B_INTER = range(9)
VECTORS, VECTOR_COUNT = 16, 9


def mm(left, right):
    return jnp.dot(left, right, preferred_element_type=F32)


def mm_tn(left, right):
    return lax.dot_general(left, right, (((0,), (0,)), ((), ())), preferred_element_type=F32)


def mm_nt(left, right):
    return lax.dot_general(left, right, (((1,), (1,)), ((), ())), preferred_element_type=F32)


def round_up(value, unit):
    return -(-value // unit) * unit


def bit(value, unit):
    if isinstance(value, int):
        return value // unit % 2
    return lax.rem(lax.div(value, jnp.int32(unit)), jnp.int32(2))


def xor(left, right, size):
    total, unit = 0, 1
    while unit < size:
        total = total + unit * ((bit(left, unit) + bit(right, unit)) % 2)
        unit *= 2
    return total


class Plane:
    def __init__(self, size, rows):
        self.size, self.pairs = size, size // 2
        self.row_parts = min(4, self.pairs)
        self.col_parts = self.pairs // self.row_parts
        self.rows = rows // self.row_parts

    def padded(self, columns):
        return 2 * round_up(round_up(columns, 256) // 2, 128 * self.col_parts)

    def piece(self, index, columns):
        width = columns // self.col_parts
        down, along = lax.rem(index, self.row_parts), lax.div(index, self.row_parts)
        if self.col_parts == 1:
            along = 0
        return down * self.rows, along * width, width


def ds(start, size, unit):
    return pl.ds(start if isinstance(start, int) else pl.multiple_of(start, unit), size)


def remote(src, dst, send, recv, device):
    return pltpu.make_async_remote_copy(
        src_ref=src, dst_ref=dst, send_sem=send, recv_sem=recv, device_id=device, device_id_type=MESH
    )


def in_turn(me, start):
    middle = (me == 1) | (me == 2)

    @pl.when(middle)
    def _():
        for j in (2, 1, 3):
            start(j)

    @pl.when(jnp.logical_not(middle))
    def _():
        for j in (1, 2, 3):
            start(j)


def greet(devices):
    barrier = pltpu.get_barrier_semaphore()
    for device in devices:
        pl.semaphore_signal(barrier, inc=1, device_id=device, device_id_type=MESH)


def meet(devices):
    pl.semaphore_wait(pltpu.get_barrier_semaphore(), len(devices))


def in_plane(side, pairs, start):
    first = [k for k in (1, 2) if k < pairs]
    rest = range(3, pairs)

    @pl.when(side == 0)
    def _():
        for k in (*first, *rest):
            start(k)

    @pl.when(side == 1)
    def _():
        for k in (*first[::-1], *rest):
            start(k)


def gelu_parts(inner):
    below = 1.0 + (ERF_P / math.sqrt(2.0)) * jnp.abs(inner)
    t = pl.reciprocal(below, approx=True)
    t = t * (2.0 - below * t)
    bell = jnp.exp(-0.5 * inner * inner)
    poly = 0.5 * ERF_A[4]
    for coeff in ERF_A[3::-1]:
        poly = poly * t + 0.5 * coeff
    tail = poly * t * bell
    below = jnp.where(inner < 0, tail, 1.0 - tail)
    return inner * below, below + inner * bell * (1.0 / math.sqrt(2.0 * math.pi))


def forward_kernel(
    groups,
    plane,
    seq_len,
    len_ref,
    tok_ref,
    cot_ref,
    w_out_ref,
    w_inter_ref,
    w_back_ref,
    w_query_ref,
    w_key_ref,
    w_value_ref,
    *refs,
):
    vector_refs, refs = refs[0:VECTOR_COUNT], refs[VECTOR_COUNT:]
    forward_body(
        groups,
        plane,
        seq_len,
        len_ref,
        tok_ref,
        cot_ref,
        (w_out_ref, w_inter_ref, w_back_ref),
        (w_query_ref, w_key_ref, w_value_ref),
        vector_refs,
        *refs,
    )


def forward_body(
    groups,
    plane,
    seq_len,
    len_ref,
    tok_ref,
    cot_ref,
    rest_refs,
    qkv_any,
    vector_any,
    cots_out,
    toks_out,
    wq_out,
    inter_out,
    back_t_out,
    out_t_out,
    vecs_out,
    placed_out,
    result_out,
    mid_low_out,
    normed1_out,
    normed2_out,
    active_out,
    slope_out,
    qkv_ref,
    expo_ref,
    inv_ref,
    ctx_ref,
    invs_ref,
    result_ref,
    mid_low_ref,
    normed1_ref,
    normed2_ref,
    active_ref,
    slope_ref,
    save_sem,
    toks,
    wq,
    rest,
    vec_rows,
    vecs,
    placed,
    inter_t,
    back_t,
    out_t,
    resid,
    qkv_refs,
    *rest_of_scratch,
):
    vector_refs = rest_of_scratch[0:VECTOR_COUNT]
    forward_steps(
        groups,
        plane,
        seq_len,
        len_ref,
        tok_ref,
        cot_ref,
        rest_refs,
        qkv_any,
        vector_any,
        (cots_out, toks_out, wq_out, inter_out, back_t_out, out_t_out, vecs_out, placed_out),
        (result_out, mid_low_out, normed1_out, normed2_out, active_out, slope_out),
        (qkv_ref, expo_ref, inv_ref, ctx_ref, invs_ref),
        (result_ref, mid_low_ref, normed1_ref, normed2_ref, active_ref, slope_ref, save_sem),
        (toks, wq, rest, vec_rows, vecs, placed, inter_t, back_t, out_t, resid),
        qkv_refs,
        vector_refs,
        *rest_of_scratch[VECTOR_COUNT:],
    )


def forward_steps(
    groups,
    plane,
    seq_len,
    len_ref,
    tok_ref,
    cot_ref,
    rest_refs,
    qkv_any,
    vector_any,
    outs,
    saved_outs,
    blocked_outs,
    saved,
    scratch,
    qkv_refs,
    vector_refs,
    local_sem,
    tok_send,
    tok_recv,
    cot_send,
    cot_recv,
    vec_send,
    vec_recv,
    q1_send,
    q1_recv,
    q2_send,
    q2_recv,
    q3_send,
    q3_recv,
    r1_send,
    r1_recv,
    r2_send,
    r2_recv,
    r3_send,
    r3_recv,
    fused=False,
):
    cots_out, toks_out, wq_out, inter_out, back_t_out, out_t_out, vecs_out, placed_out = outs
    result_out, mid_low_out, normed1_out, normed2_out, active_out, slope_out = saved_outs
    qkv_ref, expo_ref, inv_ref, ctx_ref, invs_ref = blocked_outs
    result_ref, mid_low_ref, normed1_ref, normed2_ref, active_ref, slope_ref, save_sem = saved
    toks, wq, rest, vec_rows, vecs, placed, inter_t, back_t, out_t, resid = scratch
    width, span = toks.shape[1:]
    seqs = span // seq_len
    wide = groups * width
    hidden = active_ref.shape[1]
    heads = width // HEAD_DIM
    first_mid = groups * seqs
    last = first_mid + span // BLOCK - 1
    step = pl.program_id(0)
    me, at_plane = lax.axis_index("grp"), lax.axis_index("seq")
    side, pair = lax.rem(at_plane, 2), lax.div(at_plane, 2)
    group_device = [{"grp": xor(me, j, groups)} for j in range(groups)]
    pair_device = [{"seq": xor(at_plane, 2 * k, plane.size)} for k in range(plane.pairs)]
    partner = {"seq": xor(at_plane, 1, plane.size)}
    others = range(1, groups)

    def token_copy(j, s):
        owner = xor(me, j, groups)
        return remote(
            tok_ref.at[:, ds(owner * span + s * seq_len, seq_len, seq_len)],
            toks.at[j, :, ds(s * seq_len, seq_len, seq_len)],
            tok_send.at[j, s],
            tok_recv.at[j, s],
            group_device[j],
        )

    def cot_copy(j, s):
        start = xor(me, j, groups) * span + s * seq_len
        return remote(
            cot_ref.at[:, ds(start, seq_len, seq_len)],
            cots_out.at[j, :, ds(s * seq_len, seq_len, seq_len)],
            cot_send.at[j, s],
            cot_recv.at[j, s],
            group_device[j],
        )

    def vec_copy(j):
        source = vec_rows.at[2 if j == 3 else 0]
        device = group_device[1 if j == 3 else j]
        return remote(source, vec_rows.at[j], vec_send.at[j], vec_recv.at[j], device)

    q_rows = wq.shape[1] // plane.size

    def q_own(index, s):
        return ds((s * plane.pairs + index) * q_rows, q_rows, 16)

    def q1_copy(j):
        own = q_own(pair, side)
        source = wq.at[2 if j == 3 else 0, own, :]
        device = group_device[1 if j == 3 else j]
        return remote(source, wq.at[j, own, :], q1_send.at[j], q1_recv.at[j], device)

    q_groups = (pl.ds(1, 2), pl.ds(3, 1))

    def q2_copy(late, k, index):
        part = wq.at[q_groups[late], q_own(index, side), :]
        return remote(part, part, q2_send.at[late, k], q2_recv.at[late, k], pair_device[k])

    def q3_copy(late, s):
        rows = ds(s * plane.pairs * q_rows, plane.pairs * q_rows, 16)
        part = wq.at[q_groups[late], rows, :]
        return remote(part, part, q3_send.at[late], q3_recv.at[late], partner)

    half = rest.shape[2] // 2

    def rest_piece(index):
        down, along, size = plane.piece(index, half)
        return ds(down, plane.rows, 16), ds(side * half + along, size, 128)

    def r1_copy(j):
        down, along = rest_piece(pair)
        return remote(
            rest.at[2 if j == 3 else 0, down, along],
            rest.at[j, down, along],
            r1_send.at[j],
            r1_recv.at[j],
            group_device[1 if j == 3 else j],
        )

    def r2_copy(k, index):
        down, along = rest_piece(index)
        part = rest.at[pl.ds(1, groups - 1), down, along]
        return remote(part, part, r2_send.at[k], r2_recv.at[k], pair_device[k])

    def r3_copy(s):
        part = rest.at[pl.ds(1, groups - 1), :, ds(s * half, half, 128)]
        return remote(part, part, r3_send.at[0], r3_recv.at[0], partner)

    mine = ds(me * span, span, span)
    columns = [(0, wide), (wide, hidden), (wide + hidden, hidden)]
    local_copies = [
        (tok_ref.at[:, mine], toks.at[0]),
    ]
    local_copies += [
        (ref, rest.at[0, :, pl.ds(*place)]) for ref, place in zip(rest_refs, columns)
    ]
    local_copies += [
        (toks, toks_out),
        (wq.at[:, pl.ds(0, 3 * width), :], wq_out),
        (rest.at[:, :, pl.ds(wide, hidden)], inter_out),
        (vecs, vecs_out),
        (back_t, back_t_out),
        (out_t, out_t_out),
        (placed, placed_out),
    ]
    small = [(qkv_any[i], qkv_refs.at[i]) for i in range(3)]
    small += list(zip(vector_any, vector_refs))
    local_copies += small
    saves = [
        (result_ref, result_out),
        (mid_low_ref, mid_low_out),
        (normed1_ref, normed1_out),
        (normed2_ref, normed2_out),
        (active_ref, active_out),
        (slope_ref, slope_out),
    ]

    def save(i, b):
        part = pl.ds(b * BLOCK, BLOCK)
        source, target = saves[i]
        return pltpu.make_async_copy(
            source.at[:, :, part], target.at[:, :, part], save_sem.at[i, b]
        )

    def local_copy(i):
        return pltpu.make_async_copy(*local_copies[i], local_sem.at[i])

    @pl.when(step == 0)
    def _():
        greet(group_device[1:] + pair_device[1:] + [partner])
        smalls = range(len(local_copies) - len(small), len(local_copies))
        for i in (*smalls, 0, 1, 2, 3):
            local_copy(i).start()
        meet(group_device[1:] + pair_device[1:] + [partner])
        middle = (me == 1) | (me == 2)
        pl.when(middle)(lambda: token_copy(2, 0).start())
        pl.when(jnp.logical_not(middle))(lambda: token_copy(1, 0).start())
        vecs[...] = jnp.zeros_like(vecs)
        vec_rows[0] = jnp.zeros_like(vec_rows[0])
        for i in smalls:
            local_copy(i).wait()
        for i in range(VECTOR_COUNT - 1):
            vec_rows[0, i : i + 1, 0:width] = vector_refs[i][...]
        b_inter = jnp.concatenate([vector_refs[-1][i : i + 1] for i in range(hidden // 128)], axis=1)
        for a in range(hidden // width):
            i = B_INTER + a
            vec_rows[0, i : i + 1, 0:width] = b_inter[:, a * width : (a + 1) * width]
        for i in range(3):
            wq[0, i * width : (i + 1) * width, :] = qkv_refs[i].T
        if wq.shape[1] > 3 * width:
            wq[0, 3 * width :, :] = jnp.zeros_like(wq[0, 3 * width :, :])

        def start_small(j):
            q1_copy(j).start()
            vec_copy(j).start()

        @pl.when(middle)
        def _():
            start_small(1)
            start_small(2)

        @pl.when(jnp.logical_not(middle))
        def _():
            start_small(2)
            start_small(1)

        for i in (1, 2, 3):
            local_copy(i).wait()

        @pl.when(middle)
        def _():
            r1_copy(1).start()
            r1_copy(2).start()
            for j, s in ((2, 1), (1, 0), (1, 1)):
                token_copy(j, s).start()

        @pl.when(jnp.logical_not(middle))
        def _():
            r1_copy(2).start()
            r1_copy(1).start()
            for j, s in ((1, 1), (2, 0), (2, 1)):
                token_copy(j, s).start()

        local_copy(0).wait()
        vecs[0, :, 0:VECTORS] = vec_rows[0, :, 0:width].T

    @pl.when(step == 1)
    def _():
        for j in (1, 2):
            q1_copy(j).wait_recv()
            vec_copy(j).wait_recv()
        in_plane(side, plane.pairs, lambda k: q2_copy(0, k, pair).start())
        q1_copy(3).start()
        vec_copy(3).start()
        for j in (1, 2):
            vecs[j, :, 0:VECTORS] = vec_rows[j, :, 0:width].T

    @pl.when(step == seqs)
    def _():
        for k in range(1, plane.pairs):
            q2_copy(0, k, xor(pair, k, plane.pairs)).wait_recv()
        q3_copy(0, side).start()
        r1_copy(2).wait_recv()
        middle = (me == 1) | (me == 2)
        pl.when(jnp.logical_not(middle))(lambda: token_copy(3, 0).start())
        r1_copy(3).start()
        pl.when(middle)(lambda: token_copy(3, 0).start())
        for s in range(1, seqs):
            token_copy(3, s).start()
        q3_copy(0, 1 - side).wait_recv()

    for j in others:
        for s in range(seqs):

            @pl.when(step == j * seqs + s)
            def _():
                token_copy(j, s).wait_recv()

    @pl.when(step == 2 * seqs + 1)
    def _():
        for s in range(seqs):
            cot_copy(1, s).start()
        for s in range(seqs):
            for j in (2, 3):
                cot_copy(j, s).start()
        q1_copy(3).wait_recv()
        vec_copy(3).wait_recv()
        vecs[3, :, 0:VECTORS] = vec_rows[3, :, 0:width].T
        in_plane(side, plane.pairs, lambda k: q2_copy(1, k, pair).start())
        r1_copy(1).wait_recv()
        r1_copy(3).wait_recv()
        in_plane(side, plane.pairs, lambda k: r2_copy(k, pair).start())

    @pl.when(step == 3 * seqs)
    def _():
        for k in range(1, plane.pairs):
            q2_copy(1, k, xor(pair, k, plane.pairs)).wait_recv()
        q3_copy(1, side).start()
        q3_copy(1, 1 - side).wait_recv()

    @pl.when(step == 3 * seqs + 1)
    def _():
        for k in range(1, plane.pairs):
            r2_copy(k, xor(pair, k, plane.pairs)).wait_recv()
        r3_copy(side).start()

    @pl.when(step == first_mid)
    def _():
        r3_copy(1 - side).wait_recv()
        for i in () if fused else (4, 5, 6, 7, 10):
            local_copy(i).start()
        for g in range(groups):
            inter_t[g] = rest[g, :, wide : wide + hidden].T

    @pl.when(step == first_mid + 1)
    def _():
        for g in range(groups):
            back_t[g] = rest[g, :, wide + hidden : wide + 2 * hidden].T
            out_t[:, g * width : (g + 1) * width] = rest[g, :, 0:wide].T
        for i in () if fused else (8, 9):
            local_copy(i).start()

    @pl.when(step < first_mid)
    def _():
        j, s = lax.div(step, seqs), lax.rem(step, seqs)
        at = ds(s * seq_len, seq_len, seq_len)
        length = len_ref[me * seqs + s]
        drawn = mm(wq[j, 0 : 3 * width, :], toks[j, :, at])
        vec = vecs[j]
        qkv_ref[0, 0:width, :] = (
            (drawn[0:width] + vec[:, B_QUERY : B_QUERY + 1]) * (1.0 / math.sqrt(HEAD_DIM))
        ).astype(LOW)
        qkv_ref[0, width : 2 * width, :] = drawn[width : 2 * width].astype(LOW)
        qkv_ref[0, 2 * width :, :] = (
            drawn[2 * width :] + vec[:, B_VALUE : B_VALUE + 1]
        ).astype(LOW)
        row = lax.broadcasted_iota(jnp.int32, (16, seq_len), 0)
        place = lax.broadcasted_iota(jnp.int32, (16, seq_len), 1)
        mask_rows = jnp.where((row == 0) & (place >= length), MASKED, 0.0).astype(LOW)
        one_rows = jnp.where(row == 0, 1.0, 0.0).astype(LOW)
        inv_ref[...] = jnp.zeros_like(inv_ref)
        chunks = [(h, c) for h in range(heads) for c in range(0, seq_len, BLOCK)]

        def head(h):
            low, top = h * HEAD_DIM, (h + 1) * HEAD_DIM
            queries = jnp.concatenate([qkv_ref[0, low:top, :], one_rows], axis=0)
            keys = jnp.concatenate([qkv_ref[0, width + low : width + top, :], mask_rows], axis=0)
            values = jnp.concatenate(
                [qkv_ref[0, 2 * width + low : 2 * width + top, :], one_rows], axis=0
            )
            return queries, keys.T, values

        made = [head(0)]

        def scores_of(h, c):
            if h == len(made):
                made.append(head(h))
            queries, keys, _ = made[h]
            return mm(keys, queries[:, c : c + BLOCK])

        ready = scores_of(*chunks[0])
        for i, (h, c) in enumerate(chunks):
            scores = ready
            if i + 1 < len(chunks):
                ready = scores_of(*chunks[i + 1])
            low, top = h * HEAD_DIM, (h + 1) * HEAD_DIM
            best = jnp.max(scores, axis=0, keepdims=True)
            expo = jnp.exp(scores - best).astype(LOW)
            expo_ref[0, h, :, c : c + BLOCK] = expo
            context = mm(made[h][2], expo)
            inv = 1.0 / context[HEAD_DIM : HEAD_DIM + 1]
            inv_ref[0, h : h + 1, c : c + BLOCK] = inv
            ctx_ref[0, low:top, c : c + BLOCK] = (context[0:HEAD_DIM] * inv).astype(LOW)
        placed[ds(xor(me, j, groups) * width, width, width), at] = ctx_ref[0]

    @pl.when((step >= first_mid) & (step <= last))
    def _():
        at = ds((step - first_mid) * BLOCK, BLOCK, BLOCK)

        def column(group, which):
            return vecs[group, :, which : which + 1]

        context = placed[:, at]
        total = jnp.zeros((1, BLOCK), F32)
        for j in range(groups):
            rows = toks[j, :, at].astype(F32) + (
                mm(rest[j, :, 0:wide], context) + column(j, B_OUT)
            )
            total += jnp.sum(rows, axis=0, keepdims=True)
            resid[j] = rows
        mean = total * (1.0 / wide)
        total = jnp.zeros((1, BLOCK), F32)
        for j in range(groups):
            rows = resid[j] - mean
            total += jnp.sum(rows * rows, axis=0, keepdims=True)
        inv1 = lax.rsqrt(total * (1.0 / wide) + EPS)
        for j in range(groups):
            normed = (resid[j] - mean) * inv1
            normed1_ref[j, :, at] = normed.astype(LOW)
            rows = normed * column(j, GAIN1) + column(j, SHIFT1)
            resid[j] = rows
            mid_low_ref[j, :, at] = rows.astype(LOW)
        total = jnp.zeros((1, BLOCK), F32)
        for j in range(groups):
            for a in range(0, hidden, width):
                inner = mm(inter_t[j, a : a + width, :], mid_low_ref[j, :, at]) + column(
                    j, B_INTER + a // width
                )
                active, slope = gelu_parts(inner)
                active_ref[j, a : a + width, at] = active.astype(LOW)
                slope_ref[j, a : a + width, at] = slope.astype(LOW)
            rows = resid[j] + (
                mm(rest[j, :, wide + hidden : wide + 2 * hidden], active_ref[j, :, at])
                + column(j, B_BACK)
            )
            total += jnp.sum(rows, axis=0, keepdims=True)
            resid[j] = rows
        mean = total * (1.0 / wide)
        total = jnp.zeros((1, BLOCK), F32)
        for j in range(groups):
            rows = resid[j] - mean
            total += jnp.sum(rows * rows, axis=0, keepdims=True)
        inv2 = lax.rsqrt(total * (1.0 / wide) + EPS)
        for j in range(groups):
            normed = (resid[j] - mean) * inv2
            normed2_ref[j, :, at] = normed.astype(LOW)
            result_ref[j, :, at] = (normed * column(j, GAIN2) + column(j, SHIFT2)).astype(LOW)
        invs_ref[...] = jnp.zeros_like(invs_ref)
        invs_ref[0:1, :] = inv1
        invs_ref[1:2, :] = inv2

    for b in range(span // BLOCK):

        @pl.when(step == first_mid + b)
        def _():
            for i in range(1 if fused else len(saves)):
                save(i, b).start()

    def all_sent():
        for j in others:
            q1_copy(j).wait_send()
            vec_copy(j).wait_send()
            r1_copy(j).wait_send()
            for s in range(seqs):
                token_copy(j, s).wait_send()
                cot_copy(j, s).wait_send()
        for k in range(1, plane.pairs):
            for late in (0, 1):
                q2_copy(late, k, pair).wait_send()
            r2_copy(k, pair).wait_send()
        for late in (0, 1):
            q3_copy(late, side).wait_send()
        r3_copy(side).wait_send()

    def cots_here(s):
        for j in others:
            cot_copy(j, s).wait_recv()

    def all_saved():
        for i in range(1 if fused else len(saves)):
            for b in range(span // BLOCK):
                save(i, b).wait()

    if fused:
        return cots_here, all_saved, all_sent

    @pl.when(step == last)
    def _():
        all_sent()
        for s in range(seqs):
            cots_here(s)
        all_saved()
        for i in (4, 5, 6, 7, 8, 9, 10):
            local_copy(i).wait()


def forward(sizes, lengths, tokens, cotangent, weights, vectors):
    groups, plane, seq_len, hidden = sizes
    width, total = tokens.shape
    span = total // groups
    seqs, heads, wide = span // seq_len, width // HEAD_DIM, groups * width
    attention = groups * seqs
    steps = attention + span // BLOCK
    anywhere = pl.BlockSpec(memory_space=pl.ANY)
    wq_rows = round_up(3 * width, 16 * plane.size)
    rest_columns = plane.padded(wide + 2 * hidden)

    def group_at(t):
        return lax.div(jnp.minimum(t, attention - 1), seqs)

    def seq_at(t):
        return lax.rem(jnp.minimum(t, attention - 1), seqs)

    def block_at(t):
        return jnp.maximum(t - attention, 0)

    def by_seq(rows):
        return pl.BlockSpec((1, rows, seq_len), lambda t: (group_at(t), 0, seq_at(t)))

    def low(*shape):
        return jax.ShapeDtypeStruct(shape, LOW)

    dma = pltpu.SemaphoreType.DMA
    gate = [dma((groups,)), dma((groups,))]
    gather = gate + [dma((plane.pairs,)), dma((plane.pairs,)), dma((1,)), dma((1,))]
    gather_q = gate + [dma((2, plane.pairs)), dma((2, plane.pairs)), dma((2,)), dma((2,))]
    return pl.pallas_call(
        functools.partial(forward_kernel, groups, plane, seq_len),
        grid=(steps,),
        in_specs=[pl.BlockSpec(memory_space=pltpu.SMEM)]
        + [anywhere] * (8 + VECTOR_COUNT),
        out_specs=[anywhere] * 14
        + [
            by_seq(3 * width),
            pl.BlockSpec(
                (1, heads, seq_len, seq_len),
                lambda t: (jnp.minimum(t, attention - 1), 0, 0, 0),
            ),
            by_seq(8),
            by_seq(width),
            pl.BlockSpec((8, BLOCK), lambda t: (0, block_at(t))),
        ],
        out_shape=[
            low(groups, width, span),
            low(groups, width, span),
            low(groups, 3 * width, width),
            low(groups, width, hidden),
            low(groups, hidden, width),
            low(wide, wide),
            jax.ShapeDtypeStruct((groups, width, 128), F32),
            low(wide, span),
            low(groups, width, span),
            low(groups, width, span),
            low(groups, width, span),
            low(groups, width, span),
            low(groups, hidden, span),
            low(groups, hidden, span),
            low(groups, 3 * width, span),
            low(attention, heads, seq_len, seq_len),
            jax.ShapeDtypeStruct((groups, 8, span), F32),
            low(groups, width, span),
            jax.ShapeDtypeStruct((8, span), F32),
        ],
        scratch_shapes=[
            pltpu.VMEM((groups, width, span), LOW),
            pltpu.VMEM((groups, width, span), LOW),
            pltpu.VMEM((groups, width, span), LOW),
            pltpu.VMEM((groups, width, span), LOW),
            pltpu.VMEM((groups, hidden, span), LOW),
            pltpu.VMEM((groups, hidden, span), LOW),
            dma((6, span // BLOCK)),
            pltpu.VMEM((groups, width, span), LOW),
            pltpu.VMEM((groups, wq_rows, width), LOW),
            pltpu.VMEM((groups, width, rest_columns), LOW),
            pltpu.VMEM((groups, VECTORS, round_up(width, 128)), F32),
            pltpu.VMEM((groups, width, 128), F32),
            pltpu.VMEM((wide, span), LOW),
            pltpu.VMEM((groups, hidden, width), LOW),
            pltpu.VMEM((groups, hidden, width), LOW),
            pltpu.VMEM((wide, wide), LOW),
            pltpu.VMEM((groups, width, BLOCK), F32),
            pltpu.VMEM((3, width, width), LOW),
        ]
        + [pltpu.VMEM(vector.shape, F32) for vector in vectors]
        + [
            dma((14 + VECTOR_COUNT,)),
            dma((groups, seqs)),
            dma((groups, seqs)),
        ]
        + [dma((groups, seqs)), dma((groups, seqs))]
        + gate
        + gather_q
        + gather,
        compiler_params=pltpu.CompilerParams(
            vmem_limit_bytes=VMEM_BYTES, collective_id=0, has_side_effects=True
        ),
        name="forward",
    )(lengths, tokens, cotangent, *weights, *vectors)


def lanes(block):
    folded = block[:, 0:128]
    for c in range(128, block.shape[1], 128):
        folded = folded + block[:, c : c + 128]
    return folded


def backward_kernel(
    groups,
    plane,
    seq_len,
    result_ref,
    cot_any,
    cots_any,
    placed_any,
    mid_low_any,
    normed1_any,
    normed2_any,
    invs_any,
    active_any,
    slope_any,
    qkv_any,
    expo_any,
    inv_any,
    ctx_any,
    toks_any,
    wq_any,
    inter_any,
    back_t_any,
    out_t_any,
    vecs_any,
    result_out,
    gtok_out,
    grest_out,
    gqkv_out,
    vecs_ref,
    invs_ref,
    back_t,
    inter_ref,
    out_t,
    cots_ref,
    normed1_ref,
    normed2_ref,
    qkv_ref,
    expo_ref,
    inv_ref,
    ctx_ref,
    toks_ref,
    seq_sem,
    wq_ref,
    placed_ref,
    mid_low_ref,
    active_ref,
    load_sem,
    grads,
    ffn,
    branch,
    inner,
    sums,
    stack,
    acc,
    acc_q,
    pair_got,
    plane_got,
    group_sent,
    group_got,
    total_rest,
    pair_sent_q,
    pair_got_q,
    plane_got_q,
    group_sent_q,
    group_got_q,
    total_q,
    local_sem,
    result_send,
    result_recv,
    gtok_send,
    gtok_recv,
    pair_send,
    pair_recv,
    plane_send,
    plane_recv,
    group_send,
    group_recv,
    spread_send,
    spread_recv,
    join_send,
    join_recv,
    fused_from=None,
    arrived=None,
):
    fused = fused_from is not None
    gctx = cots_ref
    width, span = gctx.shape[1:]
    seqs = span // seq_len
    wide = groups * width
    hidden = inner.shape[1]
    heads = width // HEAD_DIM
    blocks = span // BLOCK
    last = blocks + groups * seqs - 1
    step = pl.program_id(0) - (fused_from or 0)
    me, at_plane = lax.axis_index("grp"), lax.axis_index("seq")
    side, pair = lax.rem(at_plane, 2), lax.div(at_plane, 2)
    group_device = [{"grp": xor(me, j, groups)} for j in range(groups)]
    pair_device = [{"seq": xor(at_plane, 2 * k, plane.size)} for k in range(plane.pairs)]
    partner = {"seq": xor(at_plane, 1, plane.size)}
    others, mates = range(1, groups), range(1, plane.pairs)

    seq_loads = (0, 1) if fused else range(4)
    loads = [] if fused else [
        (vecs_any, vecs_ref),
        (invs_any, invs_ref),
        (back_t_any, back_t),
        (inter_any, inter_ref),
        (out_t_any, out_t),
        (wq_any, wq_ref),
        (inv_any, inv_ref),
        (placed_any, placed_ref),
        (mid_low_any, mid_low_ref),
        (active_any, active_ref),
    ]

    def load(i):
        return pltpu.make_async_copy(*loads[i], load_sem.at[i])

    away = pl.ds(1, groups - 1)
    block_loads = [] if fused else [
        (cots_any.at[away], cots_ref.at[away]),
        (normed2_any, normed2_ref),
        (slope_any, inner),
        (normed1_any, normed1_ref),
        (cot_any, cots_ref.at[0]),
    ]

    def load_block(i, b):
        part = pl.ds(b * BLOCK, BLOCK)
        source, target = block_loads[i]
        sem = load_sem.at[len(loads) + i * blocks + b]
        if i == 4:
            own = ds(me * span + b * BLOCK, BLOCK, BLOCK)
            return pltpu.make_async_copy(source.at[:, own], target.at[:, part], sem)
        return pltpu.make_async_copy(source.at[:, :, part], target.at[:, :, part], sem)

    def load_seq(i, order):
        j, s, slot = groups - 1 - order // seqs, order % seqs, order % 2
        part = pl.ds(s * seq_len, seq_len)
        source, target = (
            (qkv_any.at[j, :, part], qkv_ref),
            (expo_any.at[j * seqs + s], expo_ref),
            (ctx_any.at[j, :, part], ctx_ref),
            (toks_any.at[j, :, part], toks_ref),
        )[i]
        return pltpu.make_async_copy(source, target.at[slot], seq_sem.at[i, order])

    def result_copy(j):
        mine = result_out.at[:, ds(me * span, span, span)]
        return remote(
            result_ref.at[j], mine, result_send.at[j], result_recv.at[j], group_device[j]
        )

    def result_landing(j):
        there = result_out.at[:, ds(xor(me, j, groups) * span, span, span)]
        return remote(there, there, result_send.at[j], result_recv.at[j], group_device[j])

    def gtok_copy(j, s):
        mine = gtok_out.at[:, ds(me * span + s * seq_len, seq_len, seq_len)]
        block = gctx.at[j, :, ds(s * seq_len, seq_len, seq_len)]
        if j == 0:
            return pltpu.make_async_copy(block, mine, local_sem.at[1 + s])
        return remote(block, mine, gtok_send.at[j, s], gtok_recv.at[j, s], group_device[j])

    def gtok_landing(j, s):
        start = xor(me, j, groups) * span + s * seq_len
        there = gtok_out.at[:, ds(start, seq_len, seq_len)]
        return remote(there, there, gtok_send.at[j, s], gtok_recv.at[j, s], group_device[j])

    def buffers(number):
        if number == 0:
            return (
                acc,
                acc,
                pair_got,
                plane_got,
                group_sent,
                group_got,
                total_rest,
                pl.ds(0, groups),
            )
        return (
            acc_q,
            pair_sent_q,
            pair_got_q,
            plane_got_q,
            group_sent_q,
            group_got_q,
            total_q,
            pl.ds(number - 1, 1),
        )

    def pair_copy(number):
        full, sent, got, *_, lead = buffers(number)
        half = full.shape[2] // 2
        there = ds((1 - side) * half, half, 128) if number == 0 else pl.ds(0, half)
        return remote(
            sent.at[lead, :, there],
            got.at[lead, :, pl.ds(0, half)],
            pair_send.at[number],
            pair_recv.at[number],
            partner,
        )

    def piece_of(ref, index):
        down, along, size = plane.piece(index, ref.shape[2])
        return ds(down, plane.rows, 16), ds(along, size, 128)

    def plane_copy(number, k):
        _, _, sent, got, *_, lead = buffers(number)
        down, along = piece_of(sent, xor(pair, k, plane.pairs))
        return remote(
            sent.at[lead, down, along],
            got.at[k, lead],
            plane_send.at[number, k],
            plane_recv.at[number, k],
            pair_device[k],
        )

    def group_copy(number, j):
        sent, got = buffers(number)[4:6]
        return remote(
            sent.at[j],
            got.at[j],
            group_send.at[number, j],
            group_recv.at[number, j],
            group_device[1 if j == 3 else j],
        )

    def total_piece(total, index):
        half = total.shape[1] // 2
        down, along, size = plane.piece(index, half)
        return total.at[ds(down, plane.rows, 16), ds(side * half + along, size, 128)]

    def spread_copy(number, k, index):
        part = total_piece(buffers(number)[6], index)
        return remote(
            part, part, spread_send.at[number, k], spread_recv.at[number, k], pair_device[k]
        )

    def join_copy(number, s):
        total = buffers(number)[6]
        half = total.shape[1] // 2
        part = total.at[:, ds(s * half, half, 128)]
        return remote(part, part, join_send.at[number], join_recv.at[number], partner)

    def start_pair(number):
        full, sent, *_, lead = buffers(number)
        half = full.shape[2] // 2
        if number:
            sent[lead, :, 0:half] = full[lead, :, ds((1 - side) * half, half, 128)].astype(LOW)
        pair_copy(number).start()

    def start_plane(number):
        full, _, got, *_, lead = buffers(number)
        half = full.shape[2] // 2
        pair_copy(number).wait_recv()
        summed = full[lead, :, ds(side * half, half, 128)].astype(F32)
        summed = summed + got[lead, :, 0:half].astype(F32)
        got[lead, :, 0:half] = summed.astype(LOW)
        in_plane(side, plane.pairs, lambda k: plane_copy(number, k).start())

    def plane_sum(number):
        _, _, held, got, *_, lead = buffers(number)
        for k in mates:
            plane_copy(number, k).wait_recv()
        down, along = piece_of(held, pair)
        summed = held[lead, down, along].astype(F32)
        for k in mates:
            summed = summed + got[k, lead].astype(F32)
        return summed

    def start_group(number):
        summed = plane_sum(number)
        sent, got = buffers(number)[4:6]
        if number == 0:
            for j in range(groups):
                sent[j] = summed[j].astype(LOW)
            group_copy(0, 3).start()
            group_copy(0, 1).start()
            return
        j, summed = number - 1, summed[0]
        if j == 2:
            group_copy(1, 3).wait_recv()
            summed = summed + got[3].astype(F32)
        sent[j] = summed.astype(LOW)
        group_copy(1, j).start()

    def hand_on():
        group_copy(0, 3).wait_recv()
        group_sent[2] = (group_sent[2].astype(F32) + group_got[3].astype(F32)).astype(LOW)
        group_copy(0, 2).start()

    def start_spread(number, summed):
        got, total = buffers(number)[5:7]
        for j in (1, 2):
            group_copy(number, j).wait_recv()
            summed = summed + got[j].astype(F32)
        total_piece(total, pair)[...] = summed.astype(LOW)
        in_plane(side, plane.pairs, lambda k: spread_copy(number, k, pair).start())

    def start_join(number):
        for k in mates:
            spread_copy(number, k, xor(pair, k, plane.pairs)).wait_recv()
        join_copy(number, side).start()

    @pl.when(step == 0)
    def _():
        if not fused:
            greet(group_device[1:] + pair_device[1:] + [partner])
            for i in range(3):
                load(i).start()
            for i in range(len(block_loads)):
                load_block(i, 0).start()
            for i in (3, 4):
                load(i).start()
            meet(group_device[1:] + pair_device[1:] + [partner])
        in_turn(me, lambda j: result_copy(j).start())
        for b in range(1, blocks):
            for i in range(len(block_loads)):
                load_block(i, b).start()
        for i in range(0 if fused else 5, len(loads)):
            load(i).start()
        for i in seq_loads:
            load_seq(i, 0).start()
        for ref in (acc_q, sums):
            ref[...] = jnp.zeros_like(ref)
        for i in () if fused else range(5):
            load(i).wait()

    for b in range(blocks):

        @pl.when(step == b)
        def _():
            for i in range(len(block_loads)):
                load_block(i, b).wait()
            if fused:
                arrived(b)

    for order in range(groups * seqs):

        @pl.when(step == blocks + order)
        def _():
            for i in seq_loads:
                load_seq(i, order).wait()
                if order + 1 < groups * seqs:
                    load_seq(i, order + 1).start()

    @pl.when((step >= 0) & (step < blocks))
    def _():
        at = ds(step * BLOCK, BLOCK, BLOCK)

        def column(group, which):
            return vecs_ref[group, :, which : which + 1]

        inv1, inv2 = invs_ref[0:1, at], invs_ref[1:2, at]
        zero = jnp.zeros((1, BLOCK), F32)
        first, second = zero, zero
        for j in range(groups):
            rows = cots_ref[j, :, at].astype(F32)
            normed = normed2_ref[j, :, at].astype(F32)
            scaled = rows * column(j, GAIN2)
            first += jnp.sum(scaled, axis=0, keepdims=True)
            second += jnp.sum(scaled * normed, axis=0, keepdims=True)
            sums[GAIN2 - B_OUT, j] += lanes(rows * normed)
            sums[SHIFT2 - B_OUT, j] += lanes(rows)
        first, second = first * (1.0 / wide), second * (1.0 / wide)
        next_first, next_second = zero, zero
        for j in range(groups):
            scaled = cots_ref[j, :, at].astype(F32) * column(j, GAIN2)
            rows = inv2 * (scaled - first - normed2_ref[j, :, at].astype(F32) * second)
            low_rows = rows.astype(LOW)
            sums[B_BACK - B_OUT, j] += lanes(low_rows.astype(F32))
            ffn[j, :, at] = low_rows
            for a in range(0, hidden, width):
                inner[j, a : a + width, at] = (
                    mm(back_t[j, a : a + width, :], low_rows).astype(LOW)
                    * inner[j, a : a + width, at]
                )
            rows = rows + mm(inter_ref[j], inner[j, :, at])
            normed = normed1_ref[j, :, at].astype(F32)
            sums[GAIN1 - B_OUT, j] += lanes(rows * normed)
            sums[SHIFT1 - B_OUT, j] += lanes(rows)
            scaled = rows * column(j, GAIN1)
            next_first += jnp.sum(scaled, axis=0, keepdims=True)
            next_second += jnp.sum(scaled * normed, axis=0, keepdims=True)
            grads[j] = scaled
        first, second = next_first * (1.0 / wide), next_second * (1.0 / wide)
        for j in range(groups):
            rows = inv1 * (grads[j] - first - normed1_ref[j, :, at].astype(F32) * second)
            low_rows = rows.astype(LOW)
            branch[j * width : (j + 1) * width, at] = low_rows
            sums[0, j] += lanes(low_rows.astype(F32))
        for j in range(groups):
            there = ds(xor(me, j, groups) * width, width, width)
            gctx[j, :, at] = mm(out_t[there, :], branch[:, at]).astype(LOW)

    @pl.when(step == blocks - 1)
    def _():
        for i in range(0 if fused else 5, len(loads)):
            load(i).wait()
        lane = lax.broadcasted_iota(jnp.int32, (width, 128), 1)
        ones = jnp.ones((16, span), LOW)
        for j in range(groups):
            rows = slice(j * width, (j + 1) * width)
            acc[j, :, 0:wide] = mm_nt(branch[rows, :], placed_ref[...]).astype(LOW)
            both = mm_nt(jnp.concatenate([mid_low_ref[j], ones], axis=0), inner[j])
            acc[j, :, wide : wide + hidden] = both[0:width].astype(LOW)
            acc[j, :, wide + hidden : wide + 2 * hidden] = mm_nt(ffn[j], active_ref[j]).astype(LOW)
            small = jnp.zeros((width, 128), F32)
            for which in (B_OUT, GAIN1, SHIFT1, B_BACK, GAIN2, SHIFT2):
                added = jnp.sum(sums[which - B_OUT, j], axis=1, keepdims=True)
                small = jnp.where(lane == which, added, small)
            for a in range(0, hidden, width):
                added = both[width : width + 8, a : a + width].T[:, 0:1]
                small = jnp.where(lane == B_INTER + a // width, added, small)
            acc[j, :, wide + 2 * hidden : wide + 2 * hidden + 128] = small.astype(LOW)
        if acc.shape[2] > wide + 2 * hidden + 128:
            acc[:, :, wide + 2 * hidden + 128 :] = jnp.zeros_like(acc[:, :, wide + 2 * hidden + 128 :])
        start_pair(0)

    @pl.when(step >= blocks)
    def _():
        order = step - blocks
        j, s, slot = groups - 1 - lax.div(order, seqs), lax.rem(order, seqs), lax.rem(order, 2)
        at = ds(s * seq_len, seq_len, seq_len)
        row = lax.broadcasted_iota(jnp.int32, (16, seq_len), 0)
        minus_rows = jnp.where(row < 3, -1.0, 0.0).astype(LOW)
        chunks = [(h, c) for h in range(heads) for c in range(0, seq_len, BLOCK)]

        def context_of(low, top):
            if fused:
                start = xor(me, j, groups) * width + low
                return placed_ref[ds(start, HEAD_DIM, HEAD_DIM), at]
            return ctx_ref[slot, low:top, :]

        def head(h):
            low, top = h * HEAD_DIM, (h + 1) * HEAD_DIM
            values = jnp.concatenate(
                [qkv_ref[slot, 2 * width + low : 2 * width + top, :], minus_rows], axis=0
            )
            scaled = (gctx[j, low:top, at].astype(F32) * inv_ref[j, h : h + 1, at]).astype(LOW)
            delta = jnp.sum(
                scaled.astype(F32) * context_of(low, top).astype(F32), axis=0, keepdims=True
            )
            first = delta.astype(LOW).astype(F32)
            second = (delta - first).astype(LOW).astype(F32)
            third = delta - first - second
            parts = jnp.where(
                row == 0, first, jnp.where(row == 1, second, jnp.where(row == 2, third, 0.0))
            ).astype(LOW)
            return values.T, scaled, jnp.concatenate([scaled, parts], axis=0)

        made = [head(0)]

        def shifted_of(h, c):
            if h == len(made):
                made.append(head(h))
            return mm(made[h][0], made[h][2][:, c : c + BLOCK])

        ready = shifted_of(*chunks[0])
        for i, (h, c) in enumerate(chunks):
            shifted = ready
            if i + 1 < len(chunks):
                ready = shifted_of(*chunks[i + 1])
            low, top = h * HEAD_DIM, (h + 1) * HEAD_DIM
            part = slice(c, c + BLOCK)
            expo = expo_ref[slot, h, :, part]
            grad_s = expo * shifted.astype(LOW)
            add_k = mm_nt(qkv_ref[slot, low:top, part], grad_s)
            add_v = mm_nt(made[h][1][:, part], expo)
            grad_k = add_k if c == 0 else grad_k + add_k
            grad_v = add_v if c == 0 else grad_v + add_v
            stack[low:top, part] = (
                mm(qkv_ref[slot, width + low : width + top, :], grad_s) * (1.0 / math.sqrt(HEAD_DIM))
            ).astype(LOW)
            if c + BLOCK == seq_len:
                stack[width + low : width + top, :] = grad_k.astype(LOW)
                stack[2 * width + low : 2 * width + top, :] = grad_v.astype(LOW)
        rows = stack[...]
        gctx[j, :, at] = (
            branch[ds(j * width, width, width), at].astype(F32) + mm_tn(wq_ref[j], rows)
        ).astype(LOW)
        acc_q[j, :, 0 : 3 * width] += mm_nt(toks_ref[j, :, at] if fused else toks_ref[slot], rows)
        added = jnp.sum(rows.astype(F32), axis=1, keepdims=True)
        lane = lax.broadcasted_iota(jnp.int32, (width, 128), 1)
        acc_q[j, :, 3 * width : 3 * width + 128] += jnp.where(
            lane == B_QUERY, added[0:width], jnp.where(lane == B_VALUE, added[2 * width :], 0.0)
        )

    middle = (me == 1) | (me == 2)

    def outer_sends(j, s):
        pl.when(jnp.logical_not(middle))(lambda: gtok_copy(j, s).start())

    def middle_sends(first, second):
        for core, pieces in ((0, first), (1, second)):

            @pl.when(middle & (side == core))
            def _():
                for j, s in pieces:
                    gtok_copy(j, s).start()

    def first_step():
        outer_sends(3, 0)
        start_plane(0)

    def second_step():
        outer_sends(3, 1)
        start_pair(4)

    def third_step():
        outer_sends(2, 0)
        start_plane(4)

    def fourth_step():
        outer_sends(2, 1)
        start_pair(3)

    def fifth_step():
        middle_sends([(3, 0)], [(3, 0)])
        start_plane(3)

    def sixth_step():
        start_group(0)
        middle_sends([(1, 0)], [(3, 1)])
        start_pair(2)
        start_group(4)

    def seventh_step():
        hand_on()
        start_plane(2)
        start_group(3)
        outer_sends(1, 0)
        outer_sends(1, 1)
        middle_sends([(1, 1)], [(2, 0)])
        gtok_copy(0, 0).start()

    def eighth_step():
        start_pair(1)
        start_group(2)
        middle_sends([(3, 1), (2, 0), (2, 1)], [(2, 1), (1, 0), (1, 1)])
        gtok_copy(0, 1).start()

    for order, finish_step in enumerate(
        (
            first_step,
            second_step,
            third_step,
            fourth_step,
            fifth_step,
            sixth_step,
            seventh_step,
            eighth_step,
        )
    ):
        pl.when(step == blocks + order)(finish_step)

    @pl.when(step == last)
    def _():
        start_plane(1)
        start_spread(0, group_sent[0].astype(F32))
        start_spread(1, plane_sum(1)[0])
        start_join(0)
        start_join(1)
        join_copy(0, 1 - side).wait_recv()
        rest_done = pltpu.make_async_copy(total_rest, grest_out, local_sem.at[1 + seqs])
        rest_done.start()
        join_copy(1, 1 - side).wait_recv()
        q_done = pltpu.make_async_copy(total_q, gqkv_out, local_sem.at[2 + seqs])
        q_done.start()
        for s in range(seqs):
            gtok_copy(0, s).wait()
        for j in others:
            result_copy(j).wait_send()
            result_landing(j).wait_recv()
            for s in range(seqs):
                gtok_copy(j, s).wait_send()
                gtok_landing(j, s).wait_recv()
            for number in (0, 1):
                group_copy(number, j).wait_send()
        for number in range(1 + groups):
            pair_copy(number).wait_send()
            for k in mates:
                plane_copy(number, k).wait_send()
        for number in (0, 1):
            for k in mates:
                spread_copy(number, k, pair).wait_send()
            join_copy(number, side).wait_send()
        rest_done.wait()
        q_done.wait()


def sum_buffers(groups, width, plane, columns):
    half = columns // 2
    size = half // plane.col_parts
    return [
        pltpu.VMEM((groups, width, half), LOW),
        pltpu.VMEM((plane.pairs, groups, plane.rows, size), LOW),
        pltpu.VMEM((groups, plane.rows, size), LOW),
        pltpu.VMEM((groups, plane.rows, size), LOW),
        pltpu.VMEM((width, columns), LOW),
    ]


def sum_semaphores(groups, seqs, plane):
    dma = pltpu.SemaphoreType.DMA
    numbers = 1 + groups
    shapes = [(3 + seqs,)] + [(groups,)] * 2 + [(groups, seqs)] * 2 + [(numbers,)] * 2
    shapes += [(numbers, plane.pairs)] * 2 + [(2, groups)] * 2 + [(2, plane.pairs)] * 2 + [(2,)] * 2
    return [dma(shape) for shape in shapes]


def backward(sizes, cotangent, made):
    groups, plane, seq_len, hidden = sizes
    cots, toks, wq, inter, back_t, out_t, vecs, placed, result, mid_low, normed1, normed2 = made[0:12]
    active, slope, qkv, expo, inv, ctx, invs = made[12:]
    width, span = toks.shape[1:]
    seqs, heads, wide = span // seq_len, width // HEAD_DIM, groups * width
    blocks, attention = span // BLOCK, groups * seqs
    columns = plane.padded(wide + 2 * hidden + 128)
    columns_q = plane.padded(3 * width + 128)
    anywhere = pl.BlockSpec(memory_space=pl.ANY)

    def low(*shape):
        return jax.ShapeDtypeStruct(shape, LOW)

    dma = pltpu.SemaphoreType.DMA
    return pl.pallas_call(
        functools.partial(backward_kernel, groups, plane, seq_len),
        grid=(blocks + attention,),
        in_specs=[anywhere] * 20,
        out_specs=[anywhere] * 4,
        out_shape=[
            low(width, groups * span),
            low(width, groups * span),
            low(width, columns),
            low(width, columns_q),
        ],
        scratch_shapes=[
            pltpu.VMEM(vecs.shape, F32),
            pltpu.VMEM(invs.shape, F32),
            pltpu.VMEM(back_t.shape, LOW),
            pltpu.VMEM(inter.shape, LOW),
            pltpu.VMEM(out_t.shape, LOW),
            pltpu.VMEM(cots.shape, LOW),
            pltpu.VMEM(normed1.shape, LOW),
            pltpu.VMEM(normed2.shape, LOW),
            pltpu.VMEM((2, 3 * width, seq_len), LOW),
            pltpu.VMEM((2, heads, seq_len, seq_len), LOW),
            pltpu.VMEM(inv.shape, F32),
            pltpu.VMEM((2, width, seq_len), LOW),
            pltpu.VMEM((2, width, seq_len), LOW),
            dma((4, groups * seqs)),
            pltpu.VMEM(wq.shape, LOW),
            pltpu.VMEM(placed.shape, LOW),
            pltpu.VMEM(mid_low.shape, LOW),
            pltpu.VMEM(active.shape, LOW),
            dma((10 + 5 * blocks,)),
            pltpu.VMEM((groups, width, BLOCK), F32),
            pltpu.VMEM((groups, width, span), LOW),
            pltpu.VMEM((wide, span), LOW),
            pltpu.VMEM((groups, hidden, span), LOW),
            pltpu.VMEM((B_INTER - B_OUT, groups, width, 128), F32),
            pltpu.VMEM((3 * width, seq_len), LOW),
            pltpu.VMEM((groups, width, round_up(wide + 2 * hidden + 128, 256)), LOW),
            pltpu.VMEM((groups, width, round_up(3 * width + 128, 256)), F32),
        ]
        + sum_buffers(groups, width, plane, columns)
        + [pltpu.VMEM((groups, width, columns_q // 2), LOW)]
        + sum_buffers(groups, width, plane, columns_q)
        + sum_semaphores(groups, seqs, plane),
        compiler_params=pltpu.CompilerParams(
            vmem_limit_bytes=VMEM_BYTES, collective_id=1, has_side_effects=True
        ),
        name="backward",
    )(
        result,
        cotangent,
        cots,
        placed,
        mid_low,
        normed1,
        normed2,
        invs,
        active,
        slope,
        qkv,
        expo,
        inv,
        ctx,
        toks,
        wq,
        inter,
        back_t,
        out_t,
        vecs,
    )


def fused_kernel(groups, plane, seq_len, *refs):
    refs = list(refs)

    def take(count):
        taken = refs[0:count]
        del refs[0:count]
        return taken

    len_ref, tok_ref, cot_ref = take(3)
    rest_refs, qkv_any, vector_any = take(3), take(3), take(VECTOR_COUNT)
    result_any, qkv_hbm, expo_hbm, *outs = take(7)
    toks, wq, rest, vec_rows, vecs, placed, inter_t, back_t, out_t, resid, qkv_refs = take(11)
    vector_refs = take(VECTOR_COUNT)
    result, mid_low, normed1, normed2, active, slope, cots = take(7)
    qkv_slots, expo_slots, ctx_slot, inv_all, invs = take(5)
    save_sem, local_sem, store_sem, own_sem = take(4)
    forward_sems = take(18)
    width, span = toks.shape[1:]
    seqs, wide, hidden = span // seq_len, groups * width, active.shape[1]
    steps = groups * seqs
    offset = steps + span // BLOCK
    step = pl.program_id(0)
    me = lax.axis_index("grp")

    def stores(k):
        j, s, slot = k // seqs, k % seqs, k % 2
        there = qkv_hbm.at[j, :, pl.ds(s * seq_len, seq_len)]
        return [
            pltpu.make_async_copy(qkv_slots.at[slot], there, store_sem.at[0, k]),
            pltpu.make_async_copy(expo_slots.at[slot], expo_hbm.at[k], store_sem.at[1, k]),
        ]

    own_cot = pltpu.make_async_copy(
        cot_ref.at[:, ds(me * span, span, span)], cots.at[0], own_sem.at[0]
    )
    for k in range(steps):

        @pl.when(step == k + 2)
        def _():
            for copy in stores(k):
                copy.wait()

    at_step = jnp.minimum(step, steps - 1)
    j, s = lax.div(at_step, seqs), lax.rem(at_step, seqs)
    slot = pl.ds(lax.rem(at_step, 2), 1)
    block = jnp.minimum(jnp.maximum(step - steps, 0), span // BLOCK - 1)
    cots_here, all_saved, all_sent = forward_steps(
        groups,
        plane,
        seq_len,
        len_ref,
        tok_ref,
        cot_ref,
        rest_refs,
        qkv_any,
        vector_any,
        (cots,) + (None,) * 7,
        (result_any,) + (None,) * 5,
        (
            qkv_slots.at[slot],
            expo_slots.at[slot],
            inv_all.at[pl.ds(j, 1), :, ds(s * seq_len, seq_len, seq_len)],
            ctx_slot,
            invs.at[:, ds(block * BLOCK, BLOCK, BLOCK)],
        ),
        (result, mid_low, normed1, normed2, active, slope, save_sem),
        (toks, wq, rest, vec_rows, vecs, placed, inter_t, back_t, out_t, resid),
        qkv_refs,
        vector_refs,
        local_sem,
        *forward_sems,
        fused=True,
    )
    for k in range(steps):

        @pl.when(step == k)
        def _():
            for copy in stores(k):
                copy.start()

    pl.when(step == 1)(own_cot.start)

    pl.when(step == offset)(all_saved)

    def arrived(b):
        per_seq = seq_len // BLOCK
        if b == 0:
            own_cot.wait()
        if b % per_seq == 0:
            cots_here(b // per_seq)

    backward_kernel(
        groups,
        plane,
        seq_len,
        result_any,
        *(None,) * 9,
        qkv_hbm,
        expo_hbm,
        None,
        qkv_hbm,
        qkv_hbm,
        *(None,) * 5,
        *outs,
        vecs,
        invs,
        back_t,
        rest.at[:, :, pl.ds(wide, hidden)],
        out_t,
        cots,
        normed1,
        normed2,
        qkv_slots,
        expo_slots,
        inv_all,
        ctx_slot,
        toks,
        take(1)[0],
        wq.at[:, pl.ds(0, 3 * width), :],
        placed,
        mid_low,
        active,
        None,
        resid,
        result,
        take(1)[0],
        slope,
        *refs,
        fused_from=offset,
        arrived=arrived,
    )
    pl.when(step == offset + span // BLOCK + steps - 1)(all_sent)


def fused(sizes, lengths, tokens, cotangent, weights, vectors):
    groups, plane, seq_len, hidden = sizes
    width, total = tokens.shape
    span = total // groups
    seqs, heads, wide = span // seq_len, width // HEAD_DIM, groups * width
    attention, blocks = groups * seqs, span // BLOCK
    wq_rows = round_up(3 * width, 16 * plane.size)
    rest_columns = plane.padded(wide + 2 * hidden)
    columns = plane.padded(wide + 2 * hidden + 128)
    columns_q = plane.padded(3 * width + 128)
    anywhere = pl.BlockSpec(memory_space=pl.ANY)
    dma = pltpu.SemaphoreType.DMA

    def low(*shape):
        return jax.ShapeDtypeStruct(shape, LOW)

    def keep(*shape):
        return pltpu.VMEM(shape, LOW)

    def keep_f32(*shape):
        return pltpu.VMEM(shape, F32)

    gate = [dma((groups,)), dma((groups,))]
    by_token, by_hidden = keep(groups, width, span), keep(groups, hidden, span)
    forward_scratch = [
        by_token,
        keep(groups, wq_rows, width),
        keep(groups, width, rest_columns),
        keep_f32(groups, VECTORS, round_up(width, 128)),
        keep_f32(groups, width, 128),
        keep(wide, span),
        keep(groups, hidden, width),
        keep(groups, hidden, width),
        keep(wide, wide),
        keep_f32(groups, width, BLOCK),
        keep(3, width, width),
    ]
    forward_scratch += [keep_f32(*vector.shape) for vector in vectors]
    forward_scratch += [by_token] * 4 + [by_hidden] * 2 + [by_token]
    forward_scratch += [
        keep(2, 3 * width, seq_len),
        keep(2, heads, seq_len, seq_len),
        keep(1, width, seq_len),
        keep_f32(groups, 8, span),
        keep_f32(8, span),
        dma((6, blocks)),
        dma((14 + VECTOR_COUNT,)),
        dma((2, attention)),
        dma((1,)),
    ]
    forward_scratch += [dma((groups, seqs))] * 4 + gate
    forward_scratch += gate + [dma((2, plane.pairs)), dma((2, plane.pairs)), dma((2,)), dma((2,))]
    forward_scratch += gate + [dma((plane.pairs,)), dma((plane.pairs,)), dma((1,)), dma((1,))]
    backward_scratch = [
        dma((4, attention)),
        keep(wide, span),
        keep_f32(B_INTER - B_OUT, groups, width, 128),
        keep(3 * width, seq_len),
        keep(groups, width, round_up(wide + 2 * hidden + 128, 256)),
        keep_f32(groups, width, round_up(3 * width + 128, 256)),
    ]
    backward_scratch += sum_buffers(groups, width, plane, columns)
    backward_scratch += [keep(groups, width, columns_q // 2)]
    backward_scratch += sum_buffers(groups, width, plane, columns_q)
    backward_scratch += sum_semaphores(groups, seqs, plane)
    return pl.pallas_call(
        functools.partial(fused_kernel, groups, plane, seq_len),
        grid=(2 * (attention + blocks),),
        in_specs=[pl.BlockSpec(memory_space=pltpu.SMEM)] + [anywhere] * (8 + VECTOR_COUNT),
        out_specs=[anywhere] * 7,
        out_shape=[
            low(groups, width, span),
            low(groups, 3 * width, span),
            low(attention, heads, seq_len, seq_len),
            low(width, total),
            low(width, total),
            low(width, columns),
            low(width, columns_q),
        ],
        scratch_shapes=forward_scratch + backward_scratch,
        compiler_params=pltpu.CompilerParams(
            vmem_limit_bytes=VMEM_BYTES, collective_id=2, has_side_effects=True
        ),
        name="layer",
    )(lengths, tokens, cotangent, *weights, *vectors)


FINISH_PARTS = 4


def finish_kernel(groups, hidden, own_ref, result_ref, gtok_ref, rest_ref, qkv_ref, *refs):
    outs, refs = refs[0:17], refs[17:]
    result, gtok_low, gtok, rest, qkv, *made, in_sem, out_sem = refs
    width, rows = result_ref.shape
    wide, part, span = groups * width, width // FINISH_PARTS, rows // groups
    me = lax.axis_index("grp")
    made = dict(zip(range(2, 17), made))

    def load(i):
        if i < FINISH_PARTS:
            piece = pl.ds(i * part, part)
            return pltpu.make_async_copy(gtok_ref.at[piece], gtok_low.at[piece], in_sem.at[i])
        if i < FINISH_PARTS + 2:
            source, target = ((rest_ref, rest), (qkv_ref, qkv))[i - FINISH_PARTS]
            return pltpu.make_async_copy(source, target, in_sem.at[i])
        j = i - FINISH_PARTS - 2
        columns = ds(xor(me, j, groups) * span, span, span)
        source = result_ref.at[:, columns] if j else own_ref.at[0]
        return pltpu.make_async_copy(source, result.at[:, columns], in_sem.at[i])

    def store(i):
        return pltpu.make_async_copy(made[i], outs[i], out_sem.at[i])

    def store_tokens(i):
        piece = pl.ds(i * part, part)
        return pltpu.make_async_copy(gtok.at[piece], outs[1].at[piece], out_sem.at[17 + i])

    whole = pltpu.make_async_copy(result, outs[0], out_sem.at[0])
    for i in range(FINISH_PARTS + 2 + groups):
        load(i).start()
    for i in range(FINISH_PARTS):
        piece = pl.ds(i * part, part)
        load(i).wait()
        gtok[piece, :] = gtok_low[piece, :].astype(F32)
        store_tokens(i).start()
    load(FINISH_PARTS).wait()
    load(FINISH_PARTS + 1).wait()
    for i in range(3):
        made[2 + i][...] = qkv[:, i * width : (i + 1) * width].astype(F32)
    small = qkv[:, 3 * width : 3 * width + 128].astype(F32).T
    made[5][...] = small[B_QUERY : B_QUERY + 1]
    made[6][...] = small[B_VALUE : B_VALUE + 1]
    made[7][...] = rest[:, 0:wide].astype(F32)
    made[11][...] = rest[:, wide : wide + hidden].astype(F32)
    made[13][...] = rest[:, wide + hidden : wide + 2 * hidden].astype(F32)
    small = rest[:, wide + 2 * hidden : wide + 2 * hidden + 128].astype(F32).T
    for i, which in ((8, B_OUT), (9, GAIN1), (10, SHIFT1), (14, B_BACK), (15, GAIN2), (16, SHIFT2)):
        made[i][...] = small[which : which + 1]
    row = jnp.concatenate(
        [small[B_INTER + a : B_INTER + a + 1] for a in range(hidden // width)], axis=1
    )
    for i in range(hidden // 128):
        made[12][i : i + 1, :] = row[:, i * 128 : (i + 1) * 128]
    for i in range(2, 17):
        store(i).start()
    for j in range(groups):
        load(FINISH_PARTS + 2 + j).wait()
    whole.start()
    for i in range(FINISH_PARTS):
        store_tokens(i).wait()
    for i in range(2, 17):
        store(i).wait()
    whole.wait()


def finish(sizes, own, result, grad_tokens, grad_rest, grad_qkv):
    groups, _, _, hidden = sizes
    width, rows = result.shape
    matrix, vector = (width, groups * width), (1, width)
    shapes = [(width, width)] * 3 + [vector] * 2 + [matrix] + [vector] * 3
    shapes += [(width, hidden), (hidden // 128, 128), (width, hidden)] + [vector] * 3
    anywhere = pl.BlockSpec(memory_space=pl.ANY)
    return pl.pallas_call(
        functools.partial(finish_kernel, groups, hidden),
        in_specs=[anywhere] * 5,
        out_specs=[anywhere] * 17,
        out_shape=[jax.ShapeDtypeStruct((width, rows), LOW), jax.ShapeDtypeStruct((width, rows), F32)]
        + [jax.ShapeDtypeStruct(shape, F32) for shape in shapes],
        scratch_shapes=[
            pltpu.VMEM((width, rows), LOW),
            pltpu.VMEM((width, rows), LOW),
            pltpu.VMEM((width, rows), F32),
            pltpu.VMEM(grad_rest.shape, LOW),
            pltpu.VMEM(grad_qkv.shape, LOW),
        ]
        + [pltpu.VMEM(shape, F32) for shape in shapes]
        + [
            pltpu.SemaphoreType.DMA((FINISH_PARTS + 2 + groups,)),
            pltpu.SemaphoreType.DMA((17 + FINISH_PARTS,)),
        ],
        compiler_params=pltpu.CompilerParams(vmem_limit_bytes=VMEM_BYTES),
        name="finish",
    )(own, result, grad_tokens, grad_rest, grad_qkv)


def joined(halves, columns):
    half, whole = round_up(columns, 256) // 2, halves.shape[1]
    if 2 * half == whole:
        return halves
    return jnp.concatenate([halves[:, 0:half], halves[:, whole // 2 : whole // 2 + half]], axis=1)


def local(
    tokens,
    cotangent,
    lengths,
    w_query,
    w_key,
    w_value,
    b_query,
    b_value,
    w_out,
    b_out,
    gain_attn,
    shift_attn,
    w_inter,
    b_inter,
    w_back,
    b_back,
    gain_ffn,
    shift_ffn,
):
    width, rows = tokens.shape
    groups = lax.axis_size("grp")
    plane = Plane(lax.axis_size("seq"), width)
    seq_len = rows // lengths.shape[0]
    hidden = w_inter.shape[1]
    wide = groups * width
    sizes = (groups, plane, seq_len, hidden)

    vectors = [b_query, b_value, b_out, gain_attn, shift_attn, b_back, gain_ffn, shift_ffn, b_inter]
    weights = (w_out, w_inter, w_back, w_query, w_key, w_value)
    vectors = [vector.reshape(1, -1) for vector in vectors[:-1]] + [b_inter.reshape(-1, 128)]
    if plane.size == 8:
        own, _, _, *made = fused(sizes, lengths, tokens, cotangent, weights, vectors)
    else:
        saved = forward(sizes, lengths, tokens, cotangent, weights, vectors)
        own, made = saved[8], backward(sizes, cotangent, saved)
    result, grad_tokens, grad_rest, grad_qkv = made
    grad_rest = joined(grad_rest, wide + 2 * hidden + 128)
    grad_qkv = joined(grad_qkv, 3 * width + 128)
    outs = finish(sizes, own, result, grad_tokens, grad_rest, grad_qkv)
    return tuple(out.reshape(-1) if out.shape[0] < 8 else out for out in outs)


def solution(mesh):
    flat, matrix, vector = P("grp", "seq"), P("grp", None), P("grp")
    return jax.shard_map(
        local,
        mesh=mesh,
        in_specs=(flat, flat, P("seq"), matrix, matrix, matrix, vector, vector, matrix)
        + (vector, vector, vector, matrix, vector, matrix, vector, vector, vector),
        out_specs=(flat, flat, matrix, matrix, matrix, vector, vector, matrix, vector)
        + (vector, vector, matrix, vector, matrix, vector, vector, vector),
        check_vma=False,
    )
```

time: 832 us -> 166 us (0.20); the launches traced: 822 us -> 166 us
  waiting for transfers between devices: 346 us -> 0 us
  matrix products: 262 us -> 0 us
  Pallas kernels: 0 us -> 165 us
  blocking collectives: 92.9 us -> 0 us
  local copies, waits for them, and re-layouts: 63.8 us -> 0 us
  other arithmetic: 41.4 us -> 0 us
  between operations: 14.6 us -> 0.67 us
    dot_general x74 -> x0, matrix products: 262 us -> none  [the longest x6 57.7 us: inner_rows(): lax.dot_general(left, right, (((0,), (0,)), ((), ())), preferred_element_...]
    reduce_scatter x1 -> x0, waiting for transfers between devices: 193 us -> none  [local(): lax.psum_scatter(context_terms, 'grp', scatter_dimension=0, tiled=True)]
    pallas_call x0 -> x2, Pallas kernels: none -> 165 us  [the longest x1 161 us: fused(): pl.pallas_call(functools.partial(fused_kernel, groups, plane, seq_len), g...]
    all_gather x1 -> x0, waiting for transfers between devices: 118 us -> none  [local(): gathered = lax.all_gather(context_flat, 'grp', axis=0, tiled=True)]
    psum x5 -> x0, blocking collectives: 92.9 us -> none  [the longest x2 34.4 us: norm_back(): lax.psum((jnp.sum(scaled, axis=0), jnp.sum(scaled * normed, axis=0)), 'grp')]
    psum x1 -> x0, waiting for transfers between devices: 34.8 us -> none  [local(): lax.psum((grad_w_query, grad_w_key, grad_w_value, grad_b_query, grad_b_va...]
    unnamed x103 -> x0, local copies, waits for them, and re-layouts: 32.5 us -> none
    reduce_sum x13 -> x0, other arithmetic: 23.3 us -> none  [the longest x8 5.6 us: attend_seq(): total = jnp.sum(expo, axis=-1, keepdims=True)]
  transfers between devices with their start and end apart: 3 -> 0, of which waited for: 3 -> 0; matrix products, arithmetic and copies ran while one was open for 3% -> 0% of each run, Pallas kernels for 0% -> 0%
where the time goes in v1:
time: 166 us
  Pallas kernels  165 us (99%)
    pallas_call x1, Pallas kernels, fused(): pl.pallas_call(functools.partial(fused_kernel, groups, plane, seq_len), g...  161 us
    pallas_call x1, Pallas kernels, finish(): pl.pallas_call(functools.partial(finish_kernel, groups, hidden), in_specs...  4.31 us

profile of v1, /device:TPU:0, one launch (start us, length us, event | category | flops | bytes accessed | tf_op | source)
XLA Modules:
  0.0 165.8 jit_solution(7318205135448279935)
XLA Ops:
  0.7 160.8 %layer.1 = (bf16[4,192,1024]{2,1,0:T(8,128)(2,1)}, bf16[4,576,1024]{2,1,0:T(8,128)(2,1)}, bf16[8,3,512,512]{3,2,1,0:T(8,128)(2,1)}, bf16[192,4096]{1,0:T(8,128)(...) custom-call(s32[8]{0:T(128)} %refs_0_.1, bf16[192,4096]{1,0:T(8,128)(2,1)} %refs_1_.1, ...), custom_call_target="tpu_custom_call" | custom-call | tf_op jit(solution)/shard_map/layer/pallas_call | solution.py:1703
  161.5 4.3 %finish.1 = (bf16[192,4096]{1,0:T(8,128)(2,1)}, f32[192,4096]{1,0:T(8,128)}, f32[192,192]{1,0:T(8,128)}, f32[192,192]{1,0:T(8,128)}, f32[192,192]{1,0:T(8,128)},...) custom-call(bf16[4,192,1024]{2,1,0:T(8,128)(2,1)} %get-tuple-element, ...), custom_call_target="tpu_custom_call" | custom-call | tf_op jit(solution)/shard_map/finish/pallas_call | solution.py:1800

commit v2 on v1

--- a/solution.py
+++ b/solution.py
@@ -1753,8 +1753,12 @@
         return pltpu.make_async_copy(gtok.at[piece], outs[1].at[piece], out_sem.at[17 + i])
 
     whole = pltpu.make_async_copy(result, outs[0], out_sem.at[0])
-    for i in range(FINISH_PARTS + 2 + groups):
+    first = FINISH_PARTS + 2
+    for i in (*range(first, first + groups), *range(first)):
         load(i).start()
+    for j in range(groups):
+        load(first + j).wait()
+    whole.start()
     for i in range(FINISH_PARTS):
         piece = pl.ds(i * part, part)
         load(i).wait()
@@ -1780,9 +1784,6 @@
         made[12][i : i + 1, :] = row[:, i * 128 : (i + 1) * 128]
     for i in range(2, 17):
         store(i).start()
-    for j in range(groups):
-        load(FINISH_PARTS + 2 + j).wait()
-    whole.start()
     for i in range(FINISH_PARTS):
         store_tokens(i).wait()
     for i in range(2, 17):

time: 166 us -> 166 us (level)
  no operation moved by 1% of the time
where the time goes in v2:
time: 166 us
  Pallas kernels  165 us (99%)
    pallas_call x1, Pallas kernels, fused(): pl.pallas_call(functools.partial(fused_kernel, groups, plane, seq_len), g...  161 us
    pallas_call x1, Pallas kernels, finish(): pl.pallas_call(functools.partial(finish_kernel, groups, hidden), in_specs...  4.59 us

profile of v2, /device:TPU:0, one launch (start us, length us, event | category | flops | bytes accessed | tf_op | source)
XLA Modules:
  0.0 166.1 jit_solution(7088848565091893506)
XLA Ops:
  0.7 160.8 %layer.1 = (bf16[4,192,1024]{2,1,0:T(8,128)(2,1)}, bf16[4,576,1024]{2,1,0:T(8,128)(2,1)}, bf16[8,3,512,512]{3,2,1,0:T(8,128)(2,1)}, bf16[192,4096]{1,0:T(8,128)(...) custom-call(s32[8]{0:T(128)} %refs_0_.1, bf16[192,4096]{1,0:T(8,128)(2,1)} %refs_1_.1, ...), custom_call_target="tpu_custom_call" | custom-call | tf_op jit(solution)/shard_map/layer/pallas_call | solution.py:1703
  161.5 4.6 %finish.1 = (bf16[192,4096]{1,0:T(8,128)(2,1)}, f32[192,4096]{1,0:T(8,128)}, f32[192,192]{1,0:T(8,128)}, f32[192,192]{1,0:T(8,128)}, f32[192,192]{1,0:T(8,128)},...) custom-call(bf16[4,192,1024]{2,1,0:T(8,128)(2,1)} %get-tuple-element, ...), custom_call_target="tpu_custom_call" | custom-call | tf_op jit(solution)/shard_map/finish/pallas_call | solution.py:1801
